TPU v7x, 32 devices: a whole 2x2x4 slice. The times are simulated.
32 devices in a mesh: grp: 2 (over x), site: 16 (over z, y, core).
Axes of the slice: x: 2, y: 2, z: 4, core: 2. Of those that a mesh axis runs over, the one named last changes fastest.
Arguments:
- vectors: float32 [4, 3, 16, 288, 256], P('grp', None, 'site'), parts along dimension 0, may hold values from -6 to 6
- links: float32 [6, 2, 3, 3, 16, 288], P('grp', None, None, None, 'site'), parts along dimension 0, may hold values from -1 to 1, as said below
- momenta: int32 [4, 3], replicated, may hold values from -2 to 2
- directions: int32 [256], replicated, may hold values from 0 to 2
Outputs:
- meson: float32 [256, 8, 2, 256], P('site', 'grp'), parts along dimension 1
There are 2 independent parts, one for each index of `grp`. A program takes and returns all parts, laid end to end along the dimension named above; an argument that names none is the same for every part. Nothing has to cross between parts.
Inputs may be any that keep to these rules, and one draw needn't show every extreme that they name: Each links[k, :, :, :, t, s] holds the real and imaginary parts of a unitary 3 x 3 matrix.
All inputs are finite; a program needn't handle non-finite values.
Results may differ from a plain program's by a relative error of at most 0.0001.
Values sent between devices are 32-bit elements; how exact they have to be, the bound alone decides.
A program may use at most 128 MiB of HBM per device.

v0:
```python
import math

import jax
import jax.numpy as jnp
from jax import lax
from jax.sharding import PartitionSpec as P

TLX = 12
TLY = 12
LZ = 2


kappa = 0.08


def passed_along(block, axis, distance):
    devices = range(lax.axis_size(axis))
    route = [((i - distance) % len(devices), i) for i in devices]
    return lax.ppermute(block, axis, route)


def mat_apply(link_k, field):
    real_part = 0.0
    imag_part = 0.0
    for colour in range(3):
        u_real = link_k[0, :, colour][..., None]
        u_imag = link_k[1, :, colour][..., None]
        f_real = field[0, colour][None]
        f_imag = field[1, colour][None]
        real_part = real_part + u_real * f_real - u_imag * f_imag
        imag_part = imag_part + u_real * f_imag + u_imag * f_real
    return jnp.stack([real_part, imag_part])


def adj_apply(link_k, field):
    real_part = 0.0
    imag_part = 0.0
    for colour in range(3):
        u_real = link_k[0, colour][..., None]
        u_imag = link_k[1, colour][..., None]
        f_real = field[0, colour][None]
        f_imag = field[1, colour][None]
        real_part = real_part + u_real * f_real + u_imag * f_imag
        imag_part = imag_part + u_real * f_imag - u_imag * f_real
    return jnp.stack([real_part, imag_part])


def hop_terms(field, links, sign, tiles):
    link_x = links[0]
    back_x = adj_apply(link_x, field)
    above_x = passed_along(field[:, :, :, 0], "site", -tiles)
    below_x = passed_along(back_x[:, :, :, -1], "site", tiles)
    forward = mat_apply(
        link_x, jnp.concatenate([field[:, :, :, 1:], above_x[:, :, :, None]], axis=3)
    )
    backward = jnp.concatenate([below_x[:, :, :, None], back_x[:, :, :, :-1]], axis=3)
    terms = [forward + sign * backward]
    link_y = links[1]
    back_y = adj_apply(link_y, field)
    above_y = passed_along(field[:, :, :, :, 0], "site", -1)
    below_y = passed_along(back_y[:, :, :, :, -1], "site", 1)
    forward = mat_apply(
        link_y, jnp.concatenate([field[:, :, :, :, 1:], above_y[:, :, :, :, None]], axis=4)
    )
    backward = jnp.concatenate([below_y[:, :, :, :, None], back_y[:, :, :, :, :-1]], axis=4)
    terms.append(forward + sign * backward)
    link_z = links[2]
    forward = mat_apply(link_z, jnp.roll(field, -1, 2))
    backward = jnp.roll(adj_apply(link_z, field), 1, 2)
    terms.append(forward + sign * backward)
    return terms


def meson_fields(left_field, shifted, momenta, xs, ys, zs, lx, ly, planes, scale):
    nev = left_field.shape[-1]
    flat_v = left_field.reshape((2, 3, -1, nev))
    flat_s = shifted.reshape((2, 3, -1, nev))
    blocks = []
    for moment in range(momenta.shape[0]):
        frac = (momenta[moment, 0] * xs % lx).astype(jnp.float32) / lx
        frac = frac + (momenta[moment, 1] * ys % ly).astype(jnp.float32) / ly
        frac = frac + (momenta[moment, 2] * zs % planes).astype(jnp.float32) / planes
        theta = (2.0 * math.pi * frac).reshape(-1)
        cosine = jnp.cos(theta)[:, None]
        sine = jnp.sin(theta)[:, None]
        a_real = cosine * flat_v[0] - sine * flat_v[1]
        a_imag = -(sine * flat_v[0] + cosine * flat_v[1])
        left = jnp.stack([a_real, a_imag])
        prods = jnp.einsum("acsn,bcsm->anbm", left, flat_s, precision=lax.Precision.HIGHEST)
        re_block = prods[0, :, 0] - prods[1, :, 1]
        im_block = prods[0, :, 1] + prods[1, :, 0]
        blocks.append(jnp.stack([re_block, im_block], axis=1))
    return jnp.stack(blocks, axis=1) * scale


def on_device(vectors, links, momenta, directions):
    devices = lax.axis_size("site")
    tiles = math.isqrt(devices)
    position = lax.axis_index("site")
    tile_row = position // tiles
    tile_col = position % tiles
    nev = vectors.shape[-1]
    field = vectors[:, :, 0].reshape((2, 3, LZ, TLX, TLY, nev))
    local_links = links[:, :, :, :, 0].reshape((3, 2, 3, 3, LZ, TLX, TLY))
    masks = (directions[None, :] == jnp.arange(3, dtype=jnp.int32)[:, None]).astype(jnp.float32)
    current = field
    for repeat in range(2):
        terms = hop_terms(current, local_links, 1.0, tiles)
        current = current + kappa * (terms[0] + terms[1] + terms[2] - 6.0 * current)
    terms = hop_terms(current, local_links, -1.0, tiles)
    shifted = 0.0
    for which in range(3):
        shifted = shifted + masks[which][None, None, None, None, None, :] * terms[which]
    lx = TLX * tiles
    ly = TLY * tiles
    zs = jnp.arange(LZ, dtype=jnp.int32)[:, None, None]
    xs = (tile_row * TLX + jnp.arange(TLX, dtype=jnp.int32))[None, :, None]
    ys = (tile_col * TLY + jnp.arange(TLY, dtype=jnp.int32))[None, None, :]
    scale = 1.0 / math.sqrt(3.0 * lx * ly * LZ)
    partial_sums = meson_fields(field, shifted, momenta, xs, ys, zs, lx, ly, LZ, scale)
    return lax.psum_scatter(partial_sums, "site", scatter_dimension=0, tiled=True)


def solution(mesh):
    placed = (
        P("grp", None, "site", None, None),
        P("grp", None, None, None, "site", None),
        P(),
        P(),
    )
    return jax.shard_map(
        on_device,
        mesh=mesh,
        in_specs=placed,
        out_specs=P("site", "grp", None, None),
        check_vma=False,
    )
```

profile of v0, /device:TPU:0, one launch (start us, length us, event | category | flops | bytes accessed | tf_op | source)
XLA Modules:
  0.0 473.7 jit_solution(14543858174275118778)
XLA Ops:
  6.5 2.8 copy.52
  18.0 14.0 %multiply_add_fusion.18 = (f32[1,3,2,12,12,256]{5,0,4,3,2,1:T(1,128)S(1)}, f32[1,3,2,12,12,256]{5,0,4,3,2,1:T(1,128)S(1)}, f32[1,3,2,12,12,256]{5,0,4,3,2,1:T(1,128)S(1)}, f32[1,3,2,12,12,256]{5,0,4,3,2,1:T(1,128)S(1)}) fusion(f32[2,12,12,256]{3,2,1,0:T(8,128)} %copy.77, f32[3,2,12,12]{3,2,1,0:T(8,128)S(1)} %get-tuple-element.241, ...), kind=kLoop, calls=%fused_computation.182 | loop fusion | flops 9732096 | bytes 5349888 | tf_op jit(solution)/shard_map/add | solution.py:43
  33.1 3.0 collective-permute-start.1
  37.7 2.2 collective-permute-start
  40.6 2.3 collective-permute-start.2
  47.6 1.8 fusion.182
  49.4 1.7 fusion.184
  61.7 1.8 fusion.147
  63.4 1.9 fusion.145
  71.7 1.9 fusion.159
  73.6 2.0 fusion.157
  85.6 2.3 multiply_subtract_fusion
  88.1 8.4 %multiply_add_fusion.14 = (f32[1,3,2,12,12,256]{5,0,4,3,2,1:T(1,128)}, f32[1,3,2,12,12,256]{5,0,4,3,2,1:T(1,128)}) fusion(f32[3,2,12,12]{3,2,1,0:T(8,128)S(1)} %copy-done.93, f32[3,2,12,12]{3,2,1,0:T(8,128)S(1)} %copy-done.95, f32[3,2,12,12]{3,2,1,0:T(8,128)S(1)} %copy-done.97, f32[3,2,12,12]{3,2,1,0:T(8,128)S(1)} %copy-done.99, ...), kind=kLoop, calls=%fused_computation.174 | loop fusion | flops 4866048 | bytes 3559680 | tf_op jit(solution)/shard_map/add | solution.py:43
  96.7 3.0 multiply_subtract_fusion.21
  99.7 8.3 %multiply_subtract_fusion.16 = (f32[1,3,2,12,12,256]{5,0,4,3,2,1:T(1,128)}, f32[1,3,2,12,12,256]{5,0,4,3,2,1:T(1,128)}) fusion(f32[2,12,12,256]{3,2,1,0:T(8,128)S(1)} %copy-done.48, f32[3,2,12,12]{3,2,1,0:T(8,128)S(1)} %copy-done.125, f32[2,12,12,256]{3,2,1,0:T(8,128)S(1)} %copy-done.47, f32[3,2,12,12]{3,2,1,0:T(8,128)S(1)} %copy-done.123, ...), kind=kLoop, calls=%fused_computation.176 | loop fusion | flops 4866048 | bytes 3559680 | tf_op jit(solution)/shard_map/sub | solution.py:30
  108.7 1.9 slice.861
  110.6 1.7 slice.891
  139.3 2.7 fusion.90
  144.5 2.9 fusion.85
  149.5 7.2 %multiply_subtract_fusion.20 = (f32[1,3,2,12,12,256]{5,0,4,3,2,1:T(1,128)S(1)}, f32[1,3,2,12,12,256]{5,0,4,3,2,1:T(1,128)S(1)}) fusion(f32[2,12,12,256]{3,2,1,0:T(8,128)S(1)} %copy.65, f32[3,2,12,12]{3,2,1,0:T(8,128)S(1)} %copy-done.114, f32[2,12,12,256]{3,2,1,0:T(8,128)S(1)} %copy.63, f32[3,2,12,12]{3,2,1,0:T(8,128)S(1)} %copy-done.113, ...), kind=kLoop, calls=%fused_computation.184 | loop fusion | flops 4866048 | bytes 3559680 | tf_op jit(solution)/shard_map/sub | solution.py:30
  156.8 7.2 %multiply_subtract_fusion.18 = (f32[1,3,2,12,12,256]{5,0,4,3,2,1:T(1,128)S(1)}, f32[1,3,2,12,12,256]{5,0,4,3,2,1:T(1,128)S(1)}) fusion(f32[2,12,12,256]{3,2,1,0:T(8,128)S(1)} %copy.93, f32[3,2,12,12]{3,2,1,0:T(8,128)S(1)} %copy-done.108, f32[2,12,12,256]{3,2,1,0:T(8,128)S(1)} %copy.91, f32[3,2,12,12]{3,2,1,0:T(8,128)S(1)} %copy-done.107, ...), kind=kLoop, calls=%fused_computation.180 | loop fusion | flops 4866048 | bytes 3559680 | tf_op jit(solution)/shard_map/sub | solution.py:30
  164.1 10.6 %multiply_add_fusion.1 = f32[2,3,2,12,12,256]{5,0,4,3,2,1:T(2,128)S(1)} fusion(f32[2,3,2,12,12,256]{5,0,4,3,2,1:T(2,128)S(1)} %bitcast.451, f32[1,3,2,12,12,256]{5,0,4,3,2,1:T(1,128)S(1)} %copy-done.13, f32[1,3,2,12,12,256]{5,0,4,3,2,1:T(1,128)S(1)} %copy-done.11, f32[2,3,1,12,12,256]{5,0,4,3,2,1:T(2,128)S(1)} %fusion.63, ...), kind=kLoop, calls=%fused_computation.129 | loop fusion | flops 7962624 | bytes 15335424 | tf_op jit(solution)/shard_map/add | solution.py:109
  179.1 12.7 %multiply_add_fusion.12 = (f32[1,3,2,12,12,256]{5,0,4,3,2,1:T(1,128)S(1)}, f32[1,3,2,12,12,256]{5,0,4,3,2,1:T(1,128)S(1)}, f32[1,3,2,12,12,256]{5,0,4,3,2,1:T(1,128)S(1)}, f32[1,3,2,12,12,256]{5,0,4,3,2,1:T(1,128)S(1)}) fusion(f32[2,12,12,256]{3,2,1,0:T(8,128)S(1)} %copy.133, f32[2,12,12,256]{3,2,1,0:T(8,128)S(1)} %copy.131, ...), kind=kLoop, calls=%fused_computation.170 | loop fusion | flops 9732096 | bytes 5349888 | tf_op jit(solution)/shard_map/add | solution.py:43
  191.9 7.2 %multiply_add_fusion.8 = (f32[1,3,2,12,12,256]{5,0,4,3,2,1:T(1,128)S(1)}, f32[1,3,2,12,12,256]{5,0,4,3,2,1:T(1,128)S(1)}) fusion(f32[2,12,12,256]{3,2,1,0:T(8,128)S(1)} %copy.133, f32[2,12,12,256]{3,2,1,0:T(8,128)S(1)} %copy.131, f32[2,12,12,256]{3,2,1,0:T(8,128)S(1)} %copy.129, f32[2,12,12,256]{3,2,1,0:T(8,128)S(1)} %copy.127, ...), kind=kLoop, calls=%fused_computation.162 | loop fusion | flops 4866048 | bytes 3559680 | tf_op jit(solution)/shard_map/add | solution.py:43
  199.1 1.9 collective-permute-start.4
  201.4 1.8 collective-permute-start.6
  203.4 1.9 fusion.100
  207.3 7.2 %multiply_subtract_fusion.10 = (f32[1,3,2,12,12,256]{5,0,4,3,2,1:T(1,128)S(1)}, f32[1,3,2,12,12,256]{5,0,4,3,2,1:T(1,128)S(1)}) fusion(f32[2,12,12,256]{3,2,1,0:T(8,128)S(1)} %copy.162, f32[2,12,12,256]{3,2,1,0:T(8,128)S(1)} %copy.160, f32[2,12,12,256]{3,2,1,0:T(8,128)S(1)} %copy.158, f32[2,12,12,256]{3,2,1,0:T(8,128)S(1)} %copy.156, ...), kind=kLoop, calls=%fused_computation.164 | loop fusion | flops 4866048 | bytes 3559680 | tf_op jit(solution)/shard_map/sub | solution.py:30
  223.1 7.2 %multiply_subtract_fusion.14 = (f32[1,3,2,12,12,256]{5,0,4,3,2,1:T(1,128)S(1)}, f32[1,3,2,12,12,256]{5,0,4,3,2,1:T(1,128)S(1)}) fusion(f32[2,12,12,256]{3,2,1,0:T(8,128)S(1)} %copy.121, f32[2,12,12,256]{3,2,1,0:T(8,128)S(1)} %copy.119, f32[2,12,12,256]{3,2,1,0:T(8,128)S(1)} %copy.117, f32[2,12,12,256]{3,2,1,0:T(8,128)S(1)} %copy.115, ...), kind=kLoop, calls=%fused_computation.172 | loop fusion | flops 4866048 | bytes 3559680 | tf_op jit(solution)/shard_map/sub | solution.py:30
  230.3 7.2 %multiply_subtract_fusion.12 = (f32[1,3,2,12,12,256]{5,0,4,3,2,1:T(1,128)S(1)}, f32[1,3,2,12,12,256]{5,0,4,3,2,1:T(1,128)S(1)}) fusion(f32[2,12,12,256]{3,2,1,0:T(8,128)S(1)} %copy.148, f32[2,12,12,256]{3,2,1,0:T(8,128)S(1)} %copy.146, f32[2,12,12,256]{3,2,1,0:T(8,128)S(1)} %copy.144, f32[2,12,12,256]{3,2,1,0:T(8,128)S(1)} %copy.142, ...), kind=kLoop, calls=%fused_computation.168 | loop fusion | flops 4866048 | bytes 3559680 | tf_op jit(solution)/shard_map/sub | solution.py:30
  237.6 20.7 %multiply_add_fusion = f32[2,3,2,12,12,256]{5,0,4,3,2,1:T(2,128)S(1)} fusion(f32[1,3,2,12,12,256]{5,0,4,3,2,1:T(1,128)S(1)} %get-tuple-element.40, f32[1,3,2,12,12,256]{5,0,4,3,2,1:T(1,128)S(1)} %get-tuple-element.39, f32[2,3,1,12,12,256]{5,0,4,3,2,1:T(2,128)S(1)} %fusion.62, f32[1,3,2,12,12,256]{5,0,4,3,2,1:T(1,128)S(1)} %get-tuple-element.38, ...), kind=kLoop, calls=%fused_computation.128 | loop fusion | flops 15925248 | bytes 27131904 | tf_op jit(solution)/shard_map/add | solution.py:109
  263.4 14.0 %multiply_add_fusion.2 = (f32[1,3,2,12,12,256]{5,0,4,3,2,1:T(1,128)}, f32[1,3,2,12,12,256]{5,0,4,3,2,1:T(1,128)}, f32[1,3,2,12,12,256]{5,0,4,3,2,1:T(1,128)S(1)}, f32[1,3,2,12,12,256]{5,0,4,3,2,1:T(1,128)S(1)}) fusion(f32[2,12,12,256]{3,2,1,0:T(8,128)S(1)} %copy.175, f32[2,12,12,256]{3,2,1,0:T(8,128)S(1)} %copy.173, f32[2,12,12,256]{3,2,1,0:T(8,128)S(1)} %copy.171, ...), kind=kLoop, calls=%fused_computation.150 | loop fusion | flops 9732096 | bytes 5349888 | tf_op jit(solution)/shard_map/add | solution.py:43
  277.3 7.1 %multiply_add_fusion.6 = (f32[1,3,2,12,12,256]{5,0,4,3,2,1:T(1,128)S(1)}, f32[1,3,2,12,12,256]{5,0,4,3,2,1:T(1,128)S(1)}) fusion(f32[2,12,12,256]{3,2,1,0:T(8,128)S(1)} %copy.175, f32[2,12,12,256]{3,2,1,0:T(8,128)S(1)} %copy.173, f32[2,12,12,256]{3,2,1,0:T(8,128)S(1)} %copy.171, f32[2,12,12,256]{3,2,1,0:T(8,128)S(1)} %copy.169, ...), kind=kLoop, calls=%fused_computation.158 | loop fusion | flops 4866048 | bytes 3559680 | tf_op jit(solution)/shard_map/add | solution.py:43
  284.4 6.3 %fusion.115 = (f32[2,12,12,256]{3,2,1,0:T(8,128)}, f32[2,12,12,256]{3,2,1,0:T(8,128)}, f32[2,12,12,256]{3,2,1,0:T(8,128)}, f32[2,12,12,256]{3,2,1,0:T(8,128)}, f...) fusion(f32[2,3,1,12,12,256]{5,0,4,3,2,1:T(2,128)S(1)} %get-tuple-element.78, ...), kind=kLoop, calls=%fused_computation.335 | loop fusion | flops 442368 | bytes 3538944 | tf_op jit(solution)/shard_map/slice | solution.py:28
  292.4 1.7 mul.4936
  294.2 1.7 mul.4941
  295.9 1.7 mul.4946
  297.7 1.7 mul.4951
  301.1 4.4 collective-permute-start.10
  307.3 2.0 collective-permute-start.9
  310.2 8.1 %multiply_subtract_fusion.4 = (f32[1,3,288,256]{3,0,2,1:T(1,128)}, f32[1,3,288,256]{3,0,2,1:T(1,128)}) fusion(f32[288,256]{1,0:T(8,128)S(1)} %copy-done.66, f32[3,288]{1,0:T(4,128)S(1)} %copy-done.145, f32[288,256]{1,0:T(8,128)S(1)} %copy-done.65, f32[3,288]{1,0:T(4,128)S(1)} %copy-done.144, f32[288,256]{1,0:T(8,128)S(1)} %copy-done.64, ...), kind=kLoop, calls=%fused_computation.152 | loop fusion | flops 4866048 | bytes 3559680 | tf_op jit(solution)/shard_map/sub | solution.py:30
  318.4 2.3 fusion.1
  320.7 6.3 %fusion.125 = (f32[2,12,12,256]{3,2,1,0:T(8,128)}, f32[2,12,12,256]{3,2,1,0:T(8,128)}, f32[2,12,12,256]{3,2,1,0:T(8,128)}, f32[2,12,12,256]{3,2,1,0:T(8,128)}, f...) fusion(f32[2,3,2,12,1,256]{5,0,4,3,2,1:T(2,128)S(1)} %bitcast.493, f32[2,3,2,12,11,256]{5,0,4,3,2,1:T(2,128)S(1)} %slice-done), kind=kLoop, calls=%fused_computation.345 | loop fusion | flops 442368 | bytes 3538944 | tf_op jit(solution)/shard_map/slice | solution.py:28
  327.0 6.6 %fusion.120 = (f32[2,12,12,256]{3,2,1,0:T(8,128)}, f32[2,12,12,256]{3,2,1,0:T(8,128)}, f32[2,12,12,256]{3,2,1,0:T(8,128)}, f32[2,12,12,256]{3,2,1,0:T(8,128)}, f...) fusion(f32[2,3,2,1,12,256]{5,0,4,3,2,1:T(2,128)S(1)} %bitcast.492, f32[2,3,2,11,12,256]{5,0,4,3,2,1:T(2,128)S(1)} %slice-done.1), kind=kLoop, calls=%fused_computation.340 | loop fusion | flops 442368 | bytes 3538944 | tf_op jit(solution)/shard_map/slice | solution.py:28
  333.6 1.7 mul.4878
  335.3 1.8 mul.4883
  338.8 1.7 mul.4893
  342.3 1.7 mul.4903
  344.0 1.7 mul.4813
  345.7 1.8 mul.4818
  347.5 1.8 mul.4823
  349.3 1.8 mul.4828
  351.0 1.7 mul.4833
  352.8 1.8 mul.4838
  354.5 2.7 fusion.3
  357.4 2.8 fusion.5
  360.4 7.0 %multiply_subtract_fusion.6 = (f32[1,3,288,256]{3,0,2,1:T(1,128)S(1)}, f32[1,3,288,256]{3,0,2,1:T(1,128)S(1)}) fusion(f32[288,256]{1,0:T(8,128)S(1)} %copy-done.60, f32[3,288]{1,0:T(4,128)S(1)} %copy-done.139, f32[288,256]{1,0:T(8,128)S(1)} %copy-done.58, f32[3,288]{1,0:T(4,128)S(1)} %copy-done.138, f32[288,256]{1,0:T(8,128)S(1)} %copy-done.57, ...), kind=kLoop, calls=%fused_computation.156 | loop fusion | flops 4866048 | bytes 3559680 | tf_op jit(solution)/shard_map/sub | solution.py:30
  367.5 7.0 %multiply_subtract_fusion.8 = (f32[1,3,288,256]{3,0,2,1:T(1,128)S(1)}, f32[1,3,288,256]{3,0,2,1:T(1,128)S(1)}) fusion(f32[288,256]{1,0:T(8,128)S(1)} %copy-done.59, f32[3,288]{1,0:T(4,128)S(1)} %copy-done.136, f32[288,256]{1,0:T(8,128)S(1)} %copy-done.56, f32[3,288]{1,0:T(4,128)S(1)} %copy-done.134, f32[288,256]{1,0:T(8,128)S(1)} %copy-done.54, ...), kind=kLoop, calls=%fused_computation.160 | loop fusion | flops 4866048 | bytes 3559680 | tf_op jit(solution)/shard_map/sub | solution.py:30
  374.6 5.8 %fusion.29 = f32[2,3,288,256]{3,0,2,1:T(2,128)S(1)} fusion(f32[2,3,288,256]{3,0,2,1:T(2,128)S(1)} %bitcast.456, f32[1,3,288,256]{3,0,2,1:T(1,128)S(1)} %get-tuple-element.64, f32[1,3,288,256]{3,0,2,1:T(1,128)S(1)} %get-tuple-element.63, f32[2,3,288,256]{3,0,2,1:T(2,128)S(1)} %bitcast.455, f32[1,3,288,256]{3,0,2,1:T(1,128)S(1)} %get-tuple-element.62, ...), kind=kLoop, calls=%fused_computation.105 | loop fusion | flops 4866048 | bytes 12389376 | tf_op jit(solution)/shard_map/add | solution.py:113
  380.4 3.6 fusion.58
  385.2 3.6 fusion.55
  390.0 3.6 fusion.52
  394.7 3.9 fusion.49
  400.5 64.2 %reduce-scatter.2.cloned.1.call-done = f32[16,4,2,256]{3,0,2,1:T(8,128)} async-done(((f32[256,4,2,256]{3,0,2,1:T(8,128)}), f32[16,4,2,256]{3,0,2,1:T(8,128)}) %reduce-scatter.2.cloned.1.call-update) | async-done | bytes 131088 | tf_op jit(solution)/shard_map/reduce_scatter | solution.py:121
  (528 shorter events, 111.5 us)
Async XLA Ops:
  6.5 458.1 %reduce-scatter.2.cloned.1.call-start = ((), (), s32[]{:S(2)}) async-start(), calls=%async_computation.1 | async-start | bytes 2228224 | tf_op jit(solution)/shard_map/reduce_scatter | solution.py:121
  17.8 14.2 %copy-start.67 = (f32[3,2,12,12]{3,2,1,0:T(8,128)}, f32[3,2,12,12]{3,2,1,0:T(8,128)S(1)}, u32[]{:S(2)}) copy-start(f32[3,2,12,12]{3,2,1,0:T(8,128)S(1)} %get-tuple-element.237) | copy-start | bytes 10372
  17.8 14.2 %copy-start.69 = (f32[3,2,12,12]{3,2,1,0:T(8,128)}, f32[3,2,12,12]{3,2,1,0:T(8,128)S(1)}, u32[]{:S(2)}) copy-start(f32[3,2,12,12]{3,2,1,0:T(8,128)S(1)} %get-tuple-element.238) | copy-start | bytes 10372
  17.8 14.2 %copy-start.71 = (f32[3,2,12,12]{3,2,1,0:T(8,128)}, f32[3,2,12,12]{3,2,1,0:T(8,128)S(1)}, u32[]{:S(2)}) copy-start(f32[3,2,12,12]{3,2,1,0:T(8,128)S(1)} %get-tuple-element.239) | copy-start | bytes 10372
  17.8 14.2 %copy-start.73 = (f32[3,2,12,12]{3,2,1,0:T(8,128)}, f32[3,2,12,12]{3,2,1,0:T(8,128)S(1)}, u32[]{:S(2)}) copy-start(f32[3,2,12,12]{3,2,1,0:T(8,128)S(1)} %get-tuple-element.240) | copy-start | bytes 10372
  17.8 14.2 %copy-start.75 = (f32[3,2,12,12]{3,2,1,0:T(8,128)}, f32[3,2,12,12]{3,2,1,0:T(8,128)S(1)}, u32[]{:S(2)}) copy-start(f32[3,2,12,12]{3,2,1,0:T(8,128)S(1)} %get-tuple-element.241) | copy-start | bytes 10372
  17.9 14.2 %copy-start.77 = (f32[3,2,12,12]{3,2,1,0:T(8,128)}, f32[3,2,12,12]{3,2,1,0:T(8,128)S(1)}, u32[]{:S(2)}) copy-start(f32[3,2,12,12]{3,2,1,0:T(8,128)S(1)} %get-tuple-element.242) | copy-start | bytes 10372
  17.9 14.2 %copy-start.79 = (f32[3,2,12,12]{3,2,1,0:T(8,128)}, f32[3,2,12,12]{3,2,1,0:T(8,128)S(1)}, u32[]{:S(2)}) copy-start(f32[3,2,12,12]{3,2,1,0:T(8,128)S(1)} %get-tuple-element.187) | copy-start | bytes 10372
  17.9 14.2 %copy-start.81 = (f32[3,2,12,12]{3,2,1,0:T(8,128)}, f32[3,2,12,12]{3,2,1,0:T(8,128)S(1)}, u32[]{:S(2)}) copy-start(f32[3,2,12,12]{3,2,1,0:T(8,128)S(1)} %get-tuple-element.188) | copy-start | bytes 10372
  17.9 14.2 %copy-start.83 = (f32[3,2,12,12]{3,2,1,0:T(8,128)}, f32[3,2,12,12]{3,2,1,0:T(8,128)S(1)}, u32[]{:S(2)}) copy-start(f32[3,2,12,12]{3,2,1,0:T(8,128)S(1)} %get-tuple-element.189) | copy-start | bytes 10372
  17.9 14.2 %copy-start.85 = (f32[3,2,12,12]{3,2,1,0:T(8,128)}, f32[3,2,12,12]{3,2,1,0:T(8,128)S(1)}, u32[]{:S(2)}) copy-start(f32[3,2,12,12]{3,2,1,0:T(8,128)S(1)} %get-tuple-element.190) | copy-start | bytes 10372
  17.9 14.2 %copy-start.87 = (f32[3,2,12,12]{3,2,1,0:T(8,128)}, f32[3,2,12,12]{3,2,1,0:T(8,128)S(1)}, u32[]{:S(2)}) copy-start(f32[3,2,12,12]{3,2,1,0:T(8,128)S(1)} %get-tuple-element.191) | copy-start | bytes 10372
  17.9 14.2 %copy-start.89 = (f32[3,2,12,12]{3,2,1,0:T(8,128)}, f32[3,2,12,12]{3,2,1,0:T(8,128)S(1)}, u32[]{:S(2)}) copy-start(f32[3,2,12,12]{3,2,1,0:T(8,128)S(1)} %get-tuple-element.192) | copy-start | bytes 10372
  33.1 131.0 %collective-permute-start.1 = (f32[2,3,2,12,256]{4,0,3,2,1:T(2,128)}, f32[2,3,2,12,256]{4,0,3,2,1:T(2,128)}, u32[]{:S(2)}, u32[]{:S(2)}) collective-permute-start(f32[2,3,2,12,256]{4,0,3,2,1:T(2,128)} %maximum_bitcast_fusion.25), channel_id=1, source_target_pairs={{12,0},{13,1},{14,2},{15,3},{0,4},{1,5},{2,6},{3,7},{4,8},{5,9},{6... | collective-permute-start | bytes 442376 | tf_op jit(solution)/shard_map/ppermute | solution.py:19
  36.9 127.1 %collective-permute-start.3 = (f32[2,3,2,12,256]{4,0,3,2,1:T(2,128)}, f32[2,3,2,12,256]{4,0,3,2,1:T(2,128)}, u32[]{:S(2)}, u32[]{:S(2)}) collective-permute-start(f32[2,3,2,12,256]{4,0,3,2,1:T(2,128)} %maximum_bitcast_fusion.24), channel_id=1, source_target_pairs={{15,0},{0,1},{1,2},{2,3},{3,4},{4,5},{5,6},{6,7},{7,8},{8,9},{9,10... | collective-permute-start | bytes 442376 | tf_op jit(solution)/shard_map/ppermute | solution.py:19
  37.7 101.1 %collective-permute-start = (f32[2,3,2,12,256]{4,0,3,2,1:T(2,128)}, f32[2,3,2,12,256]{4,0,3,2,1:T(2,128)}, u32[]{:S(2)}, u32[]{:S(2)}) collective-permute-start(f32[2,3,2,12,256]{4,0,3,2,1:T(2,128)} %slice_bitcast_fusion.7), channel_id=1, source_target_pairs={{4,0},{5,1},{6,2},{7,3},{8,4},{9,5},{10,6},{11,7},{12,8},{13,9},{1... | collective-permute-start | bytes 442376 | tf_op jit(solution)/shard_map/ppermute | solution.py:19
  40.6 103.1 %collective-permute-start.2 = (f32[2,3,2,12,256]{4,0,3,2,1:T(2,128)}, f32[2,3,2,12,256]{4,0,3,2,1:T(2,128)}, u32[]{:S(2)}, u32[]{:S(2)}) collective-permute-start(f32[2,3,2,12,256]{4,0,3,2,1:T(2,128)} %slice_bitcast_fusion.6), channel_id=1, source_target_pairs={{1,0},{2,1},{3,2},{4,3},{5,4},{6,5},{7,6},{8,7},{9,8},{10,9},{11,1... | collective-permute-start | bytes 442376 | tf_op jit(solution)/shard_map/ppermute | solution.py:19
  57.0 28.6 %copy-start.2 = (f32[2,3,1,288,256]{4,3,2,1,0:T(8,128)S(1)}, f32[2,3,1,288,256]{4,3,2,1,0:T(8,128)}, u32[]{:S(2)}) copy-start(f32[2,3,1,288,256]{4,3,2,1,0:T(8,128)} %param.4) | copy-start | bytes 5308420
  88.1 8.4 %copy-start.148 = (f32[288]{0:T(512)S(1)}, f32[288]{0:T(512)}, u32[]{:S(2)}) copy-start(f32[288]{0:T(512)} %cos.41) | copy-start | bytes 3460
  88.1 8.4 %copy-start.149 = (f32[288]{0:T(512)S(1)}, f32[288]{0:T(512)}, u32[]{:S(2)}) copy-start(f32[288]{0:T(512)} %cos.43) | copy-start | bytes 3460
  88.1 8.4 %copy-start.150 = (f32[288]{0:T(512)S(1)}, f32[288]{0:T(512)}, u32[]{:S(2)}) copy-start(f32[288]{0:T(512)} %cos.45) | copy-start | bytes 3460
  88.1 8.4 %copy-start.151 = (f32[288]{0:T(512)S(1)}, f32[288]{0:T(512)}, u32[]{:S(2)}) copy-start(f32[288]{0:T(512)} %sin.41) | copy-start | bytes 3460
  88.1 8.4 %copy-start.152 = (f32[288]{0:T(512)S(1)}, f32[288]{0:T(512)}, u32[]{:S(2)}) copy-start(f32[288]{0:T(512)} %sin.43) | copy-start | bytes 3460
  88.1 8.4 %copy-start.153 = (f32[288]{0:T(512)S(1)}, f32[288]{0:T(512)}, u32[]{:S(2)}) copy-start(f32[288]{0:T(512)} %sin.45) | copy-start | bytes 3460
  99.7 8.4 %copy-start.147 = (f32[3,256]{1,0:T(4,128)S(1)}, f32[3,256]{1,0:T(4,128)}, u32[]{:S(2)}) copy-start(f32[3,256]{1,0:T(4,128)} %fusion.143) | copy-start | bytes 9220
  110.6 27.4 %copy-start.11 = (f32[1,3,2,12,12,256]{5,0,4,3,2,1:T(1,128)S(1)}, f32[1,3,2,12,12,256]{5,0,4,3,2,1:T(1,128)}, u32[]{:S(2)}) copy-start(f32[1,3,2,12,12,256]{5,0,4,3,2,1:T(1,128)} %get-tuple-element.51) | copy-start | bytes 2654212
  110.6 27.4 %copy-start.13 = (f32[1,3,2,12,12,256]{5,0,4,3,2,1:T(1,128)S(1)}, f32[1,3,2,12,12,256]{5,0,4,3,2,1:T(1,128)}, u32[]{:S(2)}) copy-start(f32[1,3,2,12,12,256]{5,0,4,3,2,1:T(1,128)} %get-tuple-element.52) | copy-start | bytes 2654212
  149.4 7.3 %copy-start.103 = (f32[3,2,12,12]{3,2,1,0:T(8,128)S(1)}, f32[3,2,12,12]{3,2,1,0:T(8,128)}, u32[]{:S(2)}) copy-start(f32[3,2,12,12]{3,2,1,0:T(8,128)} %get-tuple-element.158) | copy-start | bytes 10372
  149.4 7.3 %copy-start.104 = (f32[3,2,12,12]{3,2,1,0:T(8,128)S(1)}, f32[3,2,12,12]{3,2,1,0:T(8,128)}, u32[]{:S(2)}) copy-start(f32[3,2,12,12]{3,2,1,0:T(8,128)} %get-tuple-element.159) | copy-start | bytes 10372
  149.4 7.3 %copy-start.105 = (f32[3,2,12,12]{3,2,1,0:T(8,128)S(1)}, f32[3,2,12,12]{3,2,1,0:T(8,128)}, u32[]{:S(2)}) copy-start(f32[3,2,12,12]{3,2,1,0:T(8,128)} %get-tuple-element.160) | copy-start | bytes 10372
  149.4 7.3 %copy-start.106 = (f32[3,2,12,12]{3,2,1,0:T(8,128)S(1)}, f32[3,2,12,12]{3,2,1,0:T(8,128)}, u32[]{:S(2)}) copy-start(f32[3,2,12,12]{3,2,1,0:T(8,128)} %get-tuple-element.161) | copy-start | bytes 10372
  149.4 7.3 %copy-start.107 = (f32[3,2,12,12]{3,2,1,0:T(8,128)S(1)}, f32[3,2,12,12]{3,2,1,0:T(8,128)}, u32[]{:S(2)}) copy-start(f32[3,2,12,12]{3,2,1,0:T(8,128)} %get-tuple-element.162) | copy-start | bytes 10372
  149.4 7.3 %copy-start.108 = (f32[3,2,12,12]{3,2,1,0:T(8,128)S(1)}, f32[3,2,12,12]{3,2,1,0:T(8,128)}, u32[]{:S(2)}) copy-start(f32[3,2,12,12]{3,2,1,0:T(8,128)} %get-tuple-element.163) | copy-start | bytes 10372
  149.4 14.6 %copy-start.18 = (f32[1,3,2,12,12,256]{5,0,4,3,2,1:T(1,128)S(1)}, f32[1,3,2,12,12,256]{5,0,4,3,2,1:T(1,128)}, u32[]{:S(2)}) copy-start(f32[1,3,2,12,12,256]{5,0,4,3,2,1:T(1,128)} %get-tuple-element.50) | copy-start | bytes 2654212
  156.8 7.3 %copy-start.4 = (f32[1,3,2,12,12,256]{5,0,4,3,2,1:T(1,128)S(1)}, f32[1,3,2,12,12,256]{5,0,4,3,2,1:T(1,128)}, u32[]{:S(2)}) copy-start(f32[1,3,2,12,12,256]{5,0,4,3,2,1:T(1,128)} %copy-done.3) | copy-start | bytes 2654212
  156.8 7.3 %copy-start.6 = (f32[1,3,2,12,12,256]{5,0,4,3,2,1:T(1,128)S(1)}, f32[1,3,2,12,12,256]{5,0,4,3,2,1:T(1,128)}, u32[]{:S(2)}) copy-start(f32[1,3,2,12,12,256]{5,0,4,3,2,1:T(1,128)} %copy-done.5) | copy-start | bytes 2654212
  156.8 7.3 %copy-start.8 = (f32[1,3,2,12,12,256]{5,0,4,3,2,1:T(1,128)S(1)}, f32[1,3,2,12,12,256]{5,0,4,3,2,1:T(1,128)}, u32[]{:S(2)}) copy-start(f32[1,3,2,12,12,256]{5,0,4,3,2,1:T(1,128)} %copy-done.7) | copy-start | bytes 2654212
  156.8 7.3 %copy-start.10 = (f32[1,3,2,12,12,256]{5,0,4,3,2,1:T(1,128)S(1)}, f32[1,3,2,12,12,256]{5,0,4,3,2,1:T(1,128)}, u32[]{:S(2)}) copy-start(f32[1,3,2,12,12,256]{5,0,4,3,2,1:T(1,128)} %copy-done.9) | copy-start | bytes 2654212
  156.8 7.3 %copy-start.17 = (f32[1,3,2,12,12,256]{5,0,4,3,2,1:T(1,128)S(1)}, f32[1,3,2,12,12,256]{5,0,4,3,2,1:T(1,128)}, u32[]{:S(2)}) copy-start(f32[1,3,2,12,12,256]{5,0,4,3,2,1:T(1,128)} %get-tuple-element.49) | copy-start | bytes 2654212
  174.8 39.7 %copy-start.1 = (f32[2,3,2,12,12,256]{5,0,4,3,2,1:T(2,128)}, f32[2,3,2,12,12,256]{5,0,4,3,2,1:T(2,128)S(1)}, u32[]{:S(2)}) copy-start(f32[2,3,2,12,12,256]{5,0,4,3,2,1:T(2,128)S(1)} %multiply_add_fusion.1) | copy-start | bytes 5308420
  179.1 12.8 %copy-start.92 = (f32[3,2,12,12]{3,2,1,0:T(8,128)S(1)}, f32[3,2,12,12]{3,2,1,0:T(8,128)}, u32[]{:S(2)}) copy-start(f32[3,2,12,12]{3,2,1,0:T(8,128)} %get-tuple-element.193) | copy-start | bytes 10372
  179.1 12.8 %copy-start.94 = (f32[3,2,12,12]{3,2,1,0:T(8,128)S(1)}, f32[3,2,12,12]{3,2,1,0:T(8,128)}, u32[]{:S(2)}) copy-start(f32[3,2,12,12]{3,2,1,0:T(8,128)} %get-tuple-element.194) | copy-start | bytes 10372
  179.1 12.8 %copy-start.96 = (f32[3,2,12,12]{3,2,1,0:T(8,128)S(1)}, f32[3,2,12,12]{3,2,1,0:T(8,128)}, u32[]{:S(2)}) copy-start(f32[3,2,12,12]{3,2,1,0:T(8,128)} %get-tuple-element.195) | copy-start | bytes 10372
  179.1 12.8 %copy-start.98 = (f32[3,2,12,12]{3,2,1,0:T(8,128)S(1)}, f32[3,2,12,12]{3,2,1,0:T(8,128)}, u32[]{:S(2)}) copy-start(f32[3,2,12,12]{3,2,1,0:T(8,128)} %get-tuple-element.196) | copy-start | bytes 10372
  179.1 12.8 %copy-start.100 = (f32[3,2,12,12]{3,2,1,0:T(8,128)S(1)}, f32[3,2,12,12]{3,2,1,0:T(8,128)}, u32[]{:S(2)}) copy-start(f32[3,2,12,12]{3,2,1,0:T(8,128)} %get-tuple-element.197) | copy-start | bytes 10372
  179.1 12.8 %copy-start.102 = (f32[3,2,12,12]{3,2,1,0:T(8,128)S(1)}, f32[3,2,12,12]{3,2,1,0:T(8,128)}, u32[]{:S(2)}) copy-start(f32[3,2,12,12]{3,2,1,0:T(8,128)} %get-tuple-element.198) | copy-start | bytes 10372
  199.1 16.2 %collective-permute-start.4 = (f32[2,3,2,12,256]{4,0,3,2,1:T(2,128)S(1)}, f32[2,3,2,12,256]{4,0,3,2,1:T(2,128)S(1)}, u32[]{:S(2)}, u32[]{:S(2)}) collective-permute-start(f32[2,3,2,12,256]{4,0,3,2,1:T(2,128)S(1)} %slice_bitcast_fusion.5), channel_id=1, source_target_pairs={{4,0},{5,1},{6,2},{7,3},{8,4},{9,5},{10,6},{11,7},{12,8},{13,9},{1... | collective-permute-start | bytes 442376 | tf_op jit(solution)/shard_map/ppermute | solution.py:19
  201.1 36.5 %collective-permute-start.5 = (f32[2,3,2,12,256]{4,0,3,2,1:T(2,128)S(1)}, f32[2,3,2,12,256]{4,0,3,2,1:T(2,128)S(1)}, u32[]{:S(2)}, u32[]{:S(2)}) collective-permute-start(f32[2,3,2,12,256]{4,0,3,2,1:T(2,128)S(1)} %maximum_bitcast_fusion.23), channel_id=1, source_target_pairs={{12,0},{13,1},{14,2},{15,3},{0,4},{1,5},{2,6},{3,7},{4,8},{5,9},{6... | collective-permute-start | bytes 442376 | tf_op jit(solution)/shard_map/ppermute | solution.py:19
  201.4 17.7 %collective-permute-start.6 = (f32[2,3,2,12,256]{4,0,3,2,1:T(2,128)S(1)}, f32[2,3,2,12,256]{4,0,3,2,1:T(2,128)S(1)}, u32[]{:S(2)}, u32[]{:S(2)}) collective-permute-start(f32[2,3,2,12,256]{4,0,3,2,1:T(2,128)S(1)} %slice_bitcast_fusion.4), channel_id=1, source_target_pairs={{1,0},{2,1},{3,2},{4,3},{5,4},{6,5},{7,6},{8,7},{9,8},{10,9},{11,1... | collective-permute-start | bytes 442376 | tf_op jit(solution)/shard_map/ppermute | solution.py:19
  203.3 34.3 %collective-permute-start.7 = (f32[2,3,2,12,256]{4,0,3,2,1:T(2,128)S(1)}, f32[2,3,2,12,256]{4,0,3,2,1:T(2,128)S(1)}, u32[]{:S(2)}, u32[]{:S(2)}) collective-permute-start(f32[2,3,2,12,256]{4,0,3,2,1:T(2,128)S(1)} %maximum_bitcast_fusion.22), channel_id=1, source_target_pairs={{15,0},{0,1},{1,2},{2,3},{3,4},{4,5},{5,6},{6,7},{7,8},{8,9},{9,10... | collective-permute-start | bytes 442376 | tf_op jit(solution)/shard_map/ppermute | solution.py:19
  230.3 7.3 %copy-start.12 = (f32[1,3,2,12,12,256]{5,0,4,3,2,1:T(1,128)S(1)}, f32[1,3,2,12,12,256]{5,0,4,3,2,1:T(1,128)}, u32[]{:S(2)}) copy-start(f32[1,3,2,12,12,256]{5,0,4,3,2,1:T(1,128)} %get-tuple-element.51) | copy-start | bytes 2654212
  230.3 7.3 %copy-start.14 = (f32[1,3,2,12,12,256]{5,0,4,3,2,1:T(1,128)S(1)}, f32[1,3,2,12,12,256]{5,0,4,3,2,1:T(1,128)}, u32[]{:S(2)}) copy-start(f32[1,3,2,12,12,256]{5,0,4,3,2,1:T(1,128)} %get-tuple-element.52) | copy-start | bytes 2654212
  301.1 19.6 %collective-permute-start.10 = (f32[2,3,2,12,256]{4,0,3,2,1:T(2,128)}, f32[2,3,2,12,256]{4,0,3,2,1:T(2,128)S(1)}, u32[]{:S(2)}, u32[]{:S(2)}) collective-permute-start(f32[2,3,2,12,256]{4,0,3,2,1:T(2,128)} %slice_bitcast_fusion.2), channel_id=1, source_target_pairs={{1,0},{2,1},{3,2},{4,3},{5,4},{6,5},{7,6},{8,7},{9,8},{10,9},{11,1... | collective-permute-start | bytes 442376 | tf_op jit(solution)/shard_map/ppermute | solution.py:19
  306.3 48.2 %collective-permute-start.11 = (f32[2,3,2,12,256]{4,0,3,2,1:T(2,128)}, f32[2,3,2,12,256]{4,0,3,2,1:T(2,128)}, u32[]{:S(2)}, u32[]{:S(2)}) collective-permute-start(f32[2,3,2,12,256]{4,0,3,2,1:T(2,128)} %maximum_bitcast_fusion.20), channel_id=1, source_target_pairs={{15,0},{0,1},{1,2},{2,3},{3,4},{4,5},{5,6},{6,7},{7,8},{8,9},{9,10... | collective-permute-start | bytes 442376 | tf_op jit(solution)/shard_map/ppermute | solution.py:19
  306.3 20.6 %collective-permute-start.8 = (f32[2,3,2,12,256]{4,0,3,2,1:T(2,128)S(1)}, f32[2,3,2,12,256]{4,0,3,2,1:T(2,128)S(1)}, u32[]{:S(2)}, u32[]{:S(2)}) collective-permute-start(f32[2,3,2,12,256]{4,0,3,2,1:T(2,128)S(1)} %copy-done.127), channel_id=1, source_target_pairs={{4,0},{5,1},{6,2},{7,3},{8,4},{9,5},{10,6},{11,7},{12,8},{13,9},{1... | collective-permute-start | bytes 442376 | tf_op jit(solution)/shard_map/ppermute | solution.py:19
  307.3 50.0 %collective-permute-start.9 = (f32[2,3,2,12,256]{4,0,3,2,1:T(2,128)}, f32[2,3,2,12,256]{4,0,3,2,1:T(2,128)}, u32[]{:S(2)}, u32[]{:S(2)}) collective-permute-start(f32[2,3,2,12,256]{4,0,3,2,1:T(2,128)} %maximum_bitcast_fusion.21), channel_id=1, source_target_pairs={{12,0},{13,1},{14,2},{15,3},{0,4},{1,5},{2,6},{3,7},{4,8},{5,9},{6... | collective-permute-start | bytes 442376 | tf_op jit(solution)/shard_map/ppermute | solution.py:19
  360.3 7.1 %copy-start.49 = (f32[288,256]{1,0:T(8,128)S(1)}, f32[288,256]{1,0:T(8,128)}, u32[]{:S(2)}) copy-start(f32[288,256]{1,0:T(8,128)} %mul.4813) | copy-start | bytes 884740
  360.3 7.1 %copy-start.50 = (f32[288,256]{1,0:T(8,128)S(1)}, f32[288,256]{1,0:T(8,128)}, u32[]{:S(2)}) copy-start(f32[288,256]{1,0:T(8,128)} %mul.4818) | copy-start | bytes 884740
  360.3 7.1 %copy-start.52 = (f32[288,256]{1,0:T(8,128)S(1)}, f32[288,256]{1,0:T(8,128)}, u32[]{:S(2)}) copy-start(f32[288,256]{1,0:T(8,128)} %mul.4823) | copy-start | bytes 884740
  360.3 7.1 %copy-start.54 = (f32[288,256]{1,0:T(8,128)S(1)}, f32[288,256]{1,0:T(8,128)}, u32[]{:S(2)}) copy-start(f32[288,256]{1,0:T(8,128)} %mul.4828) | copy-start | bytes 884740
  360.3 7.1 %copy-start.56 = (f32[288,256]{1,0:T(8,128)S(1)}, f32[288,256]{1,0:T(8,128)}, u32[]{:S(2)}) copy-start(f32[288,256]{1,0:T(8,128)} %mul.4833) | copy-start | bytes 884740
  360.3 7.1 %copy-start.59 = (f32[288,256]{1,0:T(8,128)S(1)}, f32[288,256]{1,0:T(8,128)}, u32[]{:S(2)}) copy-start(f32[288,256]{1,0:T(8,128)} %mul.4838) | copy-start | bytes 884740
  360.3 7.1 %copy-start.130 = (f32[3,288]{1,0:T(4,128)S(1)}, f32[3,288]{1,0:T(4,128)}, u32[]{:S(2)}) copy-start(f32[3,288]{1,0:T(4,128)} %mul.4821) | copy-start | bytes 10372
  360.3 7.1 %copy-start.132 = (f32[3,288]{1,0:T(4,128)S(1)}, f32[3,288]{1,0:T(4,128)}, u32[]{:S(2)}) copy-start(f32[3,288]{1,0:T(4,128)} %mul.4826) | copy-start | bytes 10372
  (111 other events, 331.0 us)
Sparse Core Ops, SparseCore 0:
  400.6 64.0 reduce-scatter.1
where the time goes:
time: 483 us; the launch traced here: 474 us
  other arithmetic  234 us (48%)
  local copies, waits for them, and re-layouts  125 us (26%)
  waiting for transfers between devices  64.2 us (13%)
  starting transfers between devices  18.1 us (4%)
  between operations  17 us (4%)
  matrix products  14.7 us (3%)
    mul x81, local copies, waits for them, and re-layouts, mat_apply(): real_part = real_part + u_real * f_real - u_imag * f_imag  67.1 us
    sub x9, other arithmetic, mat_apply(): real_part = real_part + u_real * f_real - u_imag * f_imag  66.6 us
    reduce_scatter x1, waiting for transfers between devices, on_device(): lax.psum_scatter(partial_sums, 'site', scatter_dimension=0, tiled=True)  64.2 us
    add x6, other arithmetic, adj_apply(): real_part = real_part + u_real * f_real + u_imag * f_imag  63.4 us
    add x2, other arithmetic, on_device(): current = current + kappa * (terms[0] + terms[1] + terms[2] - 6.0 * current)  31.3 us
    slice x3, other arithmetic, mat_apply(): f_real = field[0, colour][None]  19.1 us
    ppermute x12, starting transfers between devices, passed_along(): return lax.ppermute(block, axis, route)  18.1 us
    dot_general x4, matrix products, meson_fields(): jnp.einsum('acsn,bcsm->anbm', left, flat_s, precision=lax.Precision.HIGHEST)  14.7 us
  transfers between devices with their start and end apart: 13, of which 1 were waited for; matrix products, arithmetic and copies ran while one was open for 43% of the time, Pallas kernels for 0%

commit v1 on v0

v1 whole, which is shorter than its diff:
```python
import functools
import math

import jax
import jax.numpy as jnp
from jax import lax
from jax.experimental import pallas as pl
from jax.experimental.pallas import tpu as pltpu
from jax.sharding import PartitionSpec as P

TLX = 12
TLY = 12
LZ = 2
YP = 16
KAPPA = 0.08
SIDE = TLX * LZ
F32 = jnp.float32
BF16 = jnp.bfloat16
MAIN = LZ * TLX * YP
HALO = 2 * LZ * YP
KHALF = 3 * MAIN + 4 * HALO


def mat(u, f):
    out = []
    for a in range(3):
        re = im = None
        for b in range(3):
            ur, ui = u[a][b]
            fr, fi = f[b]
            tr = ur * fr - ui * fi
            ti = ur * fi + ui * fr
            re = tr if re is None else re + tr
            im = ti if im is None else im + ti
        out.append((re, im))
    return out


def adj(u, f):
    out = []
    for a in range(3):
        re = im = None
        for b in range(3):
            ur, ui = u[b][a]
            fr, fi = f[b]
            tr = ur * fr + ui * fi
            ti = ur * fi - ui * fr
            re = tr if re is None else re + tr
            im = ti if im is None else im + ti
        out.append((re, im))
    return out


def kernel(n, tiles, nmom, v_ref, lk_ref, lkx_ref, lky_ref, cs_ref, dir_ref, out_ref,
           fv, fo, ft, links, send_buf, recv_buf, lh, ll, rh, rl, part, got,
           send_sem, recv_sem, rs_send, rs_recv):
    nev = v_ref.shape[-1]
    rows = nev // n
    stages = n.bit_length() - 1
    me = lax.axis_index("site")
    above_x = lax.rem(me + tiles, n)
    below_x = lax.rem(me + n - tiles, n)
    above_y = lax.rem(me + 1, n)
    below_y = lax.rem(me + n - 1, n)
    partners = []
    bits = []
    for s in range(stages):
        bit = (me // (1 << s)) % 2
        bits.append(bit)
        partners.append(me + (1 - 2 * bit) * (1 << s))

    barrier = pltpu.get_barrier_semaphore()
    greeted = [above_x, below_x, above_y, below_y] + partners
    for other in greeted:
        pl.semaphore_signal(barrier, inc=1, device_id={"site": other},
                            device_id_type=pl.DeviceIdType.MESH)

    zero_rows = jnp.zeros((YP, nev), F32)

    def fill(x, carry):
        for c in range(6):
            for z in range(LZ):
                fv[c, z, x] = zero_rows
                ft[c, z, x] = zero_rows
                fo[c, z, x] = zero_rows
        return carry

    lax.fori_loop(0, TLX + 2, fill, 0)
    for c in range(6):
        for z in range(LZ):
            for x in range(TLX):
                start = (z * TLX + x) * TLY
                fv[c, z, x + 1, 0:TLY, :] = v_ref[c, start:start + TLY, :]

    def compact(ref):
        def one(k):
            return jnp.broadcast_to(ref[:, k:k + 1], (SIDE, nev))
        return [[(one(3 * a + b), one(9 + 3 * a + b)) for b in range(3)] for a in range(3)]

    def halo_copies(rnd):
        targets = (below_x, above_x, below_y, above_y)
        return [
            pltpu.make_async_remote_copy(
                src_ref=send_buf.at[rnd, i], dst_ref=recv_buf.at[rnd, i],
                send_sem=send_sem.at[rnd, i], recv_sem=recv_sem.at[rnd, i],
                device_id={"site": targets[i]}, device_id_type=pl.DeviceIdType.MESH)
            for i in range(4)
        ]

    def pack_x(src, rnd, slot, layer):
        for c in range(6):
            for z in range(LZ):
                send_buf[rnd, slot, c, z * TLX:(z + 1) * TLX, :] = src[c, z, layer, 0:TLY, :]

    def pack_y(src, rnd, slot, row):
        for c in range(6):
            for z in range(LZ):
                send_buf[rnd, slot, c, z * TLX:(z + 1) * TLX, :] = src[c, z, 1:TLX + 1, row, :]

    def turn(rnd, slot, ref):
        u = compact(ref)
        f = [(send_buf[rnd, slot, b], send_buf[rnd, slot, 3 + b]) for b in range(3)]
        g = adj(u, f)
        for a in range(3):
            send_buf[rnd, slot, a] = g[a][0]
            send_buf[rnd, slot, 3 + a] = g[a][1]

    def pack_all(src, rnd):
        pack_x(src, rnd, 0, 1)
        pack_x(src, rnd, 1, TLX)
        turn(rnd, 1, lkx_ref)
        pack_y(src, rnd, 2, 0)
        pack_y(src, rnd, 3, TLY - 1)
        turn(rnd, 3, lky_ref)

    def unpack_all(dst, rnd):
        for c in range(6):
            for z in range(LZ):
                part_rows = slice(z * TLX, (z + 1) * TLX)
                dst[c, z, TLX + 1, 0:TLY, :] = recv_buf[rnd, 0, c, part_rows, :]
                dst[c, z, 0, 0:TLY, :] = recv_buf[rnd, 1, c, part_rows, :]
                dst[c, z, 1:TLX + 1, TLY, :] = recv_buf[rnd, 2, c, part_rows, :]
                dst[c, z, 1:TLX + 1, YP - 1, :] = recv_buf[rnd, 3, c, part_rows, :]

    pack_all(fv, 0)
    pl.semaphore_wait(barrier, len(greeted))
    first = halo_copies(0)
    for copy in first:
        copy.start()

    def spread(r, carry):
        at = pl.multiple_of(r * YP, YP)
        block = lk_ref[pl.ds(at, YP), :]
        for k in range(54):
            links[k, pl.ds(at, YP), :] = jnp.broadcast_to(block[:, k:k + 1], (YP, 128))
        return carry

    lax.fori_loop(0, LZ * (TLX + 1), spread, 0)

    def link(k, z, layer):
        at = pl.multiple_of((z * (TLX + 1) + layer) * YP, YP)
        def one(i):
            return links[18 * k + i, pl.ds(at, YP), :]
        return [[(one(3 * a + b), one(9 + 3 * a + b)) for b in range(3)] for a in range(3)]

    def load(src, z, layer, lanes):
        return [(src[b, z, layer, :, lanes], src[3 + b, z, layer, :, lanes]) for b in range(3)]

    def roll(f, shift):
        return [(pltpu.roll(r, shift, 0), pltpu.roll(i, shift, 0)) for r, i in f]

    def hops(src, z, x, lanes, k):
        f = load(src, z, x + 1, lanes)
        if k == 0:
            return (mat(link(0, z, x + 1), load(src, z, x + 2, lanes)),
                    adj(link(0, z, x), load(src, z, x, lanes)))
        if k == 1:
            u = link(1, z, x + 1)
            return mat(u, roll(f, YP - 1)), roll(adj(u, f), 1)
        other = load(src, 1 - z, x + 1, lanes)
        return mat(link(2, z, x + 1), other), adj(link(2, 1 - z, x + 1), other)

    real_row = lax.broadcasted_iota(jnp.int32, (YP, 128), 0) < TLY

    def smear(src, dst):
        def body(x, carry):
            for z in range(LZ):
                for half in range(nev // 128):
                    lanes = slice(half * 128, (half + 1) * 128)
                    total = None
                    for k in range(3):
                        fwd, bwd = hops(src, z, x, lanes, k)
                        term = [(a[0] + b[0], a[1] + b[1]) for a, b in zip(fwd, bwd)]
                        total = term if total is None else [
                            (a[0] + b[0], a[1] + b[1]) for a, b in zip(total, term)]
                    f = load(src, z, x + 1, lanes)
                    for a in range(3):
                        for p in range(2):
                            new = f[a][p] + KAPPA * (total[a][p] - 6.0 * f[a][p])
                            dst[3 * p + a, z, x + 1, :, lanes] = jnp.where(real_row, new, 0.0)
            return carry
        lax.fori_loop(0, TLX, body, 0)

    for copy in first:
        copy.wait()
    unpack_all(fv, 0)
    smear(fv, fo)
    pack_all(fo, 1)
    second = halo_copies(1)
    for copy in second:
        copy.start()

    pieces = []
    for c in range(3):
        pieces += [(c, z, x + 1) for z in range(LZ) for x in range(TLX)]
    for c in range(3):
        pieces += [(c, z, layer) for layer in (TLX + 1, 0) for z in range(LZ)]
    pieces += [None] * (2 * LZ)
    per = 128 // YP
    for chunk in range(KHALF // 128):
        mine = pieces[chunk * per:(chunk + 1) * per]
        vr = jnp.concatenate([zero_rows if q is None else fv[q[0], q[1], q[2]] for q in mine], 0)
        vi = jnp.concatenate([zero_rows if q is None else fv[3 + q[0], q[1], q[2]] for q in mine], 0)
        vr = vr.T
        vi = vi.T
        lanes = slice(chunk * 128, (chunk + 1) * 128)
        lanes_i = slice(KHALF + chunk * 128, KHALF + (chunk + 1) * 128)
        for m in range(nmom):
            co = cs_ref[2 * m:2 * m + 1, lanes]
            si = cs_ref[2 * m + 1:2 * m + 2, lanes]
            ar = co * vr - si * vi
            ai = -(si * vr + co * vi)
            for a, where_to in ((ar, lanes), (ai, lanes_i)):
                hi = a.astype(BF16)
                lh[m * nev:(m + 1) * nev, where_to] = hi
                ll[m * nev:(m + 1) * nev, where_to] = (a - hi.astype(F32)).astype(BF16)

    for copy in second:
        copy.wait()
    unpack_all(fo, 1)
    smear(fo, ft)

    def put(row, col, value):
        hi = value.astype(BF16)
        rh[pl.ds(row, YP), col] = hi
        rl[pl.ds(row, YP), col] = (value - hi.astype(F32)).astype(BF16)

    def put_complex(row, half, s):
        left = slice(half * 128, (half + 1) * 128)
        right = slice(nev + half * 128, nev + (half + 1) * 128)
        put(row, left, s[0])
        put(row, right, s[1])
        put(row + KHALF, left, -s[1])
        put(row + KHALF, right, s[0])

    def displace(x, carry):
        for z in range(LZ):
            for half in range(nev // 128):
                lanes = slice(half * 128, (half + 1) * 128)
                which = dir_ref[0:1, lanes]
                diffs = []
                for k in range(3):
                    fwd, bwd = hops(ft, z, x, lanes, k)
                    diffs.append([(a[0] - b[0], a[1] - b[1]) for a, b in zip(fwd, bwd)])
                for c in range(3):
                    s = tuple(jnp.where(which == 0, diffs[0][c][p],
                                        jnp.where(which == 1, diffs[1][c][p], diffs[2][c][p]))
                              for p in range(2))
                    put_complex(pl.multiple_of(c * MAIN + (z * TLX + x) * YP, YP), half, s)
        return carry

    lax.fori_loop(0, TLX, displace, 0)
    for z in range(LZ):
        for half in range(nev // 128):
            lanes = slice(half * 128, (half + 1) * 128)
            on_x = dir_ref[0:1, lanes] == 0
            high = adj(link(0, z, TLX), load(ft, z, TLX, lanes))
            low = load(ft, z, 1, lanes)
            for c in range(3):
                base = 3 * MAIN + c * HALO + z * YP
                put_complex(base, half, tuple(jnp.where(on_x, -high[c][p], 0.0) for p in range(2)))
                put_complex(base + LZ * YP, half,
                            tuple(jnp.where(on_x, low[c][p], 0.0) for p in range(2)))
    zero_tail = jnp.zeros((HALO, 2 * nev), BF16)
    for base in (KHALF - HALO, 2 * KHALF - HALO):
        rh[base:base + HALO, :] = zero_tail
        rl[base:base + HALO, :] = zero_tail

    def reversed_bits(o):
        return sum(((o >> s) & 1) << (stages - 1 - s) for s in range(stages))

    got_at = [0]
    for s in range(stages):
        got_at.append(got_at[-1] + (n >> (s + 1)))
    bases = [0]
    for s in range(stages):
        bases.append(bases[-1] + bits[s] * (n >> (s + 1)))
    copies = {}

    def launch(m, s):
        size = n >> (s + 1)
        copies[m, s] = pltpu.make_async_remote_copy(
            src_ref=part.at[m, pl.ds(bases[s] + (1 - bits[s]) * size, size)],
            dst_ref=got.at[m, pl.ds(got_at[s], size)],
            send_sem=rs_send.at[m, s], recv_sem=rs_recv.at[m, s],
            device_id={"site": partners[s]}, device_id_type=pl.DeviceIdType.MESH)
        copies[m, s].start()

    for tick in range(nmom + stages):
        if tick < nmom:
            m = tick
            take = slice(m * nev, (m + 1) * nev)
            prod = jnp.dot(lh[take, :], rh[...], preferred_element_type=F32)
            prod = prod + jnp.dot(lh[take, :], rl[...], preferred_element_type=F32)
            prod = prod + jnp.dot(ll[take, :], rh[...], preferred_element_type=F32)
            for o in range(n):
                part[m, reversed_bits(o)] = prod[o * rows:(o + 1) * rows, :]
            launch(m, 0)
        for s in range(stages - 1, -1, -1):
            m = tick - 1 - s
            if 0 <= m < nmom:
                copies[m, s].wait()
                size = n >> (s + 1)
                keep = pl.ds(bases[s + 1], size)
                summed = part[m, keep] + got[m, got_at[s]:got_at[s] + size]
                if s + 1 < stages:
                    part[m, keep] = summed
                    launch(m, s + 1)
                else:
                    out_ref[m] = summed[0]


def on_device(vectors, links, momenta, directions):
    n = lax.axis_size("site")
    tiles = math.isqrt(n)
    position = lax.axis_index("site")
    tile_row = position // tiles
    tile_col = position % tiles
    nev = vectors.shape[-1]
    nmom = momenta.shape[0]
    rows = nev // n
    stages = n.bit_length() - 1
    lx = TLX * tiles
    ly = TLY * tiles
    field = vectors.reshape((6, LZ * TLX * TLY, nev))
    local = links.reshape((3, 18, LZ, TLX, TLY))
    unit = jnp.concatenate([jnp.eye(3, dtype=F32).reshape(9), jnp.zeros(9, F32)])
    lkx = jnp.pad(local[0, :, :, TLX - 1].reshape(18, SIDE).T, ((0, 0), (0, 110)))
    lky = jnp.pad(local[1, :, :, :, TLY - 1].reshape(18, SIDE).T, ((0, 0), (0, 110)))
    flat = local.reshape(54, LZ, TLX, TLY).transpose(1, 2, 3, 0)
    zeros18 = jnp.zeros(18, F32)
    edge_y = jnp.concatenate([zeros18, unit, zeros18])
    edge_x = jnp.concatenate([unit, zeros18, zeros18])
    flat = jnp.concatenate([
        flat, jnp.zeros((LZ, TLX, YP - TLY - 1, 54), F32),
        jnp.broadcast_to(edge_y, (LZ, TLX, 1, 54))], axis=2)
    flat = jnp.concatenate([jnp.broadcast_to(edge_x, (LZ, 1, YP, 54)), flat], axis=1)
    lk = jnp.pad(flat.reshape(LZ * (TLX + 1) * YP, 54), ((0, 0), (0, 74)))

    ypos = jnp.arange(YP, dtype=jnp.int32)
    ypos = jnp.where(ypos == YP - 1, -1, ypos)
    gy = (tile_col * TLY + ypos)[None, None, :]
    xs = jnp.concatenate([jnp.arange(TLX), jnp.array([TLX, -1])]).astype(jnp.int32)
    gx = (tile_row * TLX + xs)[None, :, None]
    gx = gx + TLX * (gy >= ly).astype(jnp.int32) - TLX * (gy < 0).astype(jnp.int32)
    gx = jnp.mod(gx, lx)
    gy = jnp.mod(gy, ly)
    gz = jnp.arange(LZ, dtype=jnp.int32)[:, None, None]
    mom = momenta[:, :, None, None, None]
    frac = (mom[:, 0] * gx % lx).astype(F32) / lx
    frac = frac + (mom[:, 1] * gy % ly).astype(F32) / ly
    frac = frac + (mom[:, 2] * gz % LZ).astype(F32) / LZ
    theta = 2.0 * math.pi * frac
    scale = 1.0 / math.sqrt(3.0 * lx * ly * LZ)
    cs = jnp.stack([jnp.cos(theta), jnp.sin(theta)], axis=1) * scale
    main = cs[:, :, :, :TLX].reshape(2 * nmom, MAIN)
    halo = cs[:, :, :, TLX:].transpose(0, 1, 3, 2, 4).reshape(2 * nmom, HALO)
    cs = jnp.concatenate([main] * 3 + [halo] * 4, axis=1)

    vmem = pl.BlockSpec(memory_space=pltpu.VMEM)
    ext = pltpu.VMEM((6, LZ, TLX + 2, YP, nev), F32)
    out = pl.pallas_call(
        functools.partial(kernel, n, tiles, nmom),
        out_shape=jax.ShapeDtypeStruct((nmom, rows, 2 * nev), F32),
        in_specs=[vmem] * 6,
        out_specs=vmem,
        scratch_shapes=[
            ext, ext, ext,
            pltpu.VMEM((54, LZ * (TLX + 1) * YP, 128), F32),
            pltpu.VMEM((2, 4, 6, SIDE, nev), F32),
            pltpu.VMEM((2, 4, 6, SIDE, nev), F32),
            pltpu.VMEM((nmom * nev, 2 * KHALF), BF16),
            pltpu.VMEM((nmom * nev, 2 * KHALF), BF16),
            pltpu.VMEM((2 * KHALF, 2 * nev), BF16),
            pltpu.VMEM((2 * KHALF, 2 * nev), BF16),
            pltpu.VMEM((nmom, n, rows, 2 * nev), F32),
            pltpu.VMEM((nmom, n, rows, 2 * nev), F32),
            pltpu.SemaphoreType.DMA((2, 4)),
            pltpu.SemaphoreType.DMA((2, 4)),
            pltpu.SemaphoreType.DMA((nmom, stages)),
            pltpu.SemaphoreType.DMA((nmom, stages)),
        ],
        compiler_params=pltpu.CompilerParams(
            collective_id=0, has_side_effects=True, vmem_limit_bytes=60 * 1024 * 1024),
    )(field, lk, lkx, lky, cs, directions.reshape(1, nev))
    return out.reshape(nmom, rows, 2, nev).transpose(1, 0, 2, 3)


def solution(mesh):
    placed = (
        P("grp", None, "site", None, None),
        P("grp", None, None, None, "site", None),
        P(),
        P(),
    )
    return jax.shard_map(
        on_device,
        mesh=mesh,
        in_specs=placed,
        out_specs=P("site", "grp", None, None),
        check_vma=False,
    )
```

time: 483 us -> 92.4 us (0.19); the launches traced: 474 us -> 92.2 us
  other arithmetic: 234 us -> 2.64 us
  local copies, waits for them, and re-layouts: 125 us -> 8.42 us
  Pallas kernels: 0 us -> 81 us
  waiting for transfers between devices: 64.2 us -> 0 us
  starting transfers between devices: 18.1 us -> 0 us
  between operations: 17 us -> 0.12 us
  matrix products: 14.7 us -> 0 us
    add x13 -> x2, other arithmetic: 102 us -> 0.75 us  [the longest x1 0.66 us: on_device(): gx = (tile_row * TLX + xs)[None, :, None]]
    pallas_call x0 -> x1, Pallas kernels: none -> 81 us  [on_device(): pl.pallas_call(functools.partial(kernel, n, tiles, nmom), out_shape=jax.S...]
    mul x104 -> x0, local copies, waits for them, and re-layouts: 73.5 us -> none  [the longest x81 67.1 us: mat_apply(): real_part = real_part + u_real * f_real - u_imag * f_imag]
    sub x15 -> x0, other arithmetic: 72.2 us -> none  [the longest x9 66.6 us: mat_apply(): real_part = real_part + u_real * f_real - u_imag * f_imag]
    reduce_scatter x1 -> x0, waiting for transfers between devices: 64.2 us -> none  [on_device(): lax.psum_scatter(partial_sums, 'site', scatter_dimension=0, tiled=True)]
    slice x55 -> x3, local copies, waits for them, and re-layouts: 24.9 us -> 1.39 us  [the longest x1 1.01 us: on_device(): frac = (mom[:, 0] * gx % lx).astype(F32) / lx]
    slice x3 -> x0, other arithmetic: 19.1 us -> none  [mat_apply(): f_real = field[0, colour][None]]
    ppermute x12 -> x0, starting transfers between devices: 18.1 us -> none  [passed_along(): return lax.ppermute(block, axis, route)]
  transfers between devices with their start and end apart: 13 -> 0, of which waited for: 1 -> 0; matrix products, arithmetic and copies ran while one was open for 43% -> 0% of each run, Pallas kernels for 0% -> 0%
where the time goes in v1:
time: 92.4 us; the launch traced here: 92.2 us
  Pallas kernels  81 us (88%)
  local copies, waits for them, and re-layouts  8.42 us (9%)
  other arithmetic  2.64 us (3%)
    pallas_call x1, Pallas kernels, on_device(): pl.pallas_call(functools.partial(kernel, n, tiles, nmom), out_shape=jax.S...  81 us

profile of v1, /device:TPU:0, one launch (start us, length us, event | category | flops | bytes accessed | tf_op | source)
XLA Modules:
  0.0 92.2 jit_solution(7518865594485706860)
XLA Ops:
  0.0 0.7 broadcast_add_fusion
  0.7 1.0 %slice_reduce_fusion.4 = (s32[4]{0:T(128)S(1)}, s32[4]{0:T(128)S(1)}, s32[4]{0:T(128)S(1)}) fusion(s32[4,3,1,1,1]{1,0,4,3,2:T(4,128)} %bitcast.19), kind=kLoop, calls=%fused_computation.37 | loop fusion | bytes 96 | tf_op jit(solution)/shard_map/slice | solution.py:370
  1.7 0.1 fusion.12
  1.8 0.1 fusion.15
  1.9 0.1 reshape.294
  1.9 0.1 pad_maximum_fusion
  2.0 0.1 add_select_fusion.1
  2.1 0.1 pad.18.clone
  2.2 0.1 fusion.4
  2.3 0.3 fusion.1
  2.7 0.1 reshape.290
  2.8 0.1 reshape.291
  2.9 0.7 concatenate.34.cs_ref
  3.6 1.1 %reduce = f32[3,2,3,3,288]{4,3,2,1,0:T(4,128)S(1)} reduce(f32[3,2,3,3,1,288]{5,4,3,2,1,0:T(1,128)} %param.6, f32[]{:T(128)} %constant.112), dimensions={4}, to_apply=%param.6.reduce_sub_computation | reduce | bytes 124420 | tf_op args[1]
  4.7 0.8 reshape.289
  5.5 0.3 slice_reduce_fusion
  5.8 0.1 slice_reduce_fusion.1
  5.9 0.1 reshape.295
  5.9 0.1 reshape.296
  6.0 0.1 copy.22
  6.1 0.6 pad.13.lky_ref
  6.7 0.1 copy.21
  6.8 0.6 pad.12.lkx_ref
  7.4 0.8 reshape_reshape.3
  8.2 0.6 copy.16
  8.7 0.1 maximum_maximum_fusion
  8.8 0.7 pad.11.lk_ref
  9.5 81.0 %shard_map.55 = f32[4,16,512]{2,1,0:T(8,128)} custom-call(f32[6,288,256]{2,1,0:T(8,128)} %bitcast.14, f32[416,128]{1,0:T(8,128)} %pad.11.lk_ref, f32[24,128]{1,0:T(8,128)} %pad.12.lkx_ref, f32[24,128]{1,0:T(8,128)} %pad.13.lky_ref, f32[8,1408]{1,0:T(8,128)} %concatenate.34.cs_ref, s32[1,256]{1,0:T(1,128)} %bitcast.20), custom_call_target="tpu_custom_call" | custom-call | tf_op jit(solution)/shard_map/pallas_call | solution.py:382
  90.5 1.0 %reshape.293 = f32[4,16,2,256]{3,2,1,0:T(2,128)S(1)} reshape(f32[4,16,512]{2,1,0:T(8,128)} %shard_map.55) | data formatting | bytes 262144 | tf_op jit(solution)/shard_map/reshape | solution.py:406
  91.5 0.7 copy.24
  (12 shorter events, 0.1 us)

commit v2 on v1

v2 whole, which is shorter than its diff:
```python
import functools
import math

import jax
import jax.numpy as jnp
import numpy as np
from jax import lax
from jax.experimental import pallas as pl
from jax.experimental.pallas import tpu as pltpu
from jax.sharding import PartitionSpec as P

TLX = 12
TLY = 12
LZ = 2
YP = 16
KAPPA = 0.08
SIDE = TLX * LZ
F32 = jnp.float32
BF16 = jnp.bfloat16
MAIN = LZ * TLX * YP
HALO = 2 * LZ * YP
KHALF = 3 * MAIN + 4 * HALO


def mat(u, f):
    out = []
    for a in range(3):
        re = im = None
        for b in range(3):
            ur, ui = u[a][b]
            fr, fi = f[b]
            tr = ur * fr - ui * fi
            ti = ur * fi + ui * fr
            re = tr if re is None else re + tr
            im = ti if im is None else im + ti
        out.append((re, im))
    return out


def adj(u, f):
    out = []
    for a in range(3):
        re = im = None
        for b in range(3):
            ur, ui = u[b][a]
            fr, fi = f[b]
            tr = ur * fr + ui * fi
            ti = ur * fi - ui * fr
            re = tr if re is None else re + tr
            im = ti if im is None else im + ti
        out.append((re, im))
    return out


def kernel(n, tiles, nmom, v_ref, lk_ref, pos_ref, mom_ref, dir_ref, out_ref,
           fv, fo, ft, links, lkw, lkt, lkp, lkx, lky, cs, send_buf, recv_buf, lh, ll, rh, rl,
           part, got, send_sem, recv_sem, rs_send, rs_recv):
    nev = v_ref.shape[-1]
    halves = nev // 128
    rows = nev // n
    stages = n.bit_length() - 1
    me = lax.axis_index("site")
    above_x = lax.rem(me + tiles, n)
    below_x = lax.rem(me + n - tiles, n)
    above_y = lax.rem(me + 1, n)
    below_y = lax.rem(me + n - 1, n)
    partners = []
    bits = []
    for s in range(stages):
        bit = (me // (1 << s)) % 2
        bits.append(bit)
        partners.append(me + (1 - 2 * bit) * (1 << s))

    barrier = pltpu.get_barrier_semaphore()
    greeted = [above_x, below_x, above_y, below_y] + partners
    for other in greeted:
        pl.semaphore_signal(barrier, inc=1, device_id={"site": other},
                            device_id_type=pl.DeviceIdType.MESH)

    def lanes_of(half):
        return slice(half * 128, (half + 1) * 128)

    lkw[...] = jnp.zeros_like(lkw)
    lkw[0:54, 0:SIDE * TLY] = lk_ref[...]
    lkt[...] = lkw[...].T
    lane = lax.broadcasted_iota(jnp.int32, (YP, 128), 1)
    row = lax.broadcasted_iota(jnp.int32, (YP, 128), 0)
    unit_x = jnp.where((lane == 0) | (lane == 4) | (lane == 8), 1.0, 0.0)
    unit_y = jnp.where(((lane == 18) | (lane == 22) | (lane == 26)) & (row == YP - 1), 1.0, 0.0)
    for z in range(LZ):
        lkp[z, 0] = unit_x
        for x in range(TLX):
            first_row = (z * TLX + x) * TLY
            lkp[z, x + 1] = unit_y
            lkp[z, x + 1, 0:TLY, :] = lkt[first_row:first_row + TLY, :]
        last = (z + 1) * TLX * TLY - TLY
        lkx[z * TLX:(z + 1) * TLX, :] = lkt[last:last + TLY, :]
    lky[...] = lkt[pl.ds(TLY - 1, SIDE, stride=TLY), :]

    def compact(ref, k):
        def one(i):
            return jnp.broadcast_to(ref[:, 18 * k + i:18 * k + i + 1], (SIDE, 128))
        return [[(one(3 * a + b), one(9 + 3 * a + b)) for b in range(3)] for a in range(3)]

    def halo_copies(rnd, half):
        targets = (below_x, above_x, below_y, above_y)
        return [
            pltpu.make_async_remote_copy(
                src_ref=send_buf.at[rnd, half, i], dst_ref=recv_buf.at[rnd, half, i],
                send_sem=send_sem.at[rnd, half, i], recv_sem=recv_sem.at[rnd, half, i],
                device_id={"site": targets[i]}, device_id_type=pl.DeviceIdType.MESH)
            for i in range(4)
        ]

    def turn(rnd, half, slot, ref, k):
        u = compact(ref, k)
        f = [(send_buf[rnd, half, slot, b], send_buf[rnd, half, slot, 3 + b]) for b in range(3)]
        g = adj(u, f)
        for a in range(3):
            send_buf[rnd, half, slot, a] = g[a][0]
            send_buf[rnd, half, slot, 3 + a] = g[a][1]

    def pack_given(half):
        lanes = lanes_of(half)
        for c in range(6):
            p, b = c // 3, c % 3
            for z in range(LZ):
                at = z * TLX * TLY
                last = at + TLX * TLY - TLY
                to = slice(z * TLX, (z + 1) * TLX)
                send_buf[0, half, 0, c, to, :] = v_ref[p, b, 0, at:at + TLY, lanes]
                send_buf[0, half, 1, c, to, :] = v_ref[p, b, 0, last:last + TLY, lanes]
                for x in range(TLX):
                    i = z * TLX + x
                    send_buf[0, half, 2, c, i:i + 1, :] = v_ref[p, b, 0, at + x * TLY:at + x * TLY + 1, lanes]
                    y = at + x * TLY + TLY - 1
                    send_buf[0, half, 3, c, i:i + 1, :] = v_ref[p, b, 0, y:y + 1, lanes]
        turn(0, half, 1, lkx, 0)
        turn(0, half, 3, lky, 1)

    def pack(src, rnd, half):
        lanes = lanes_of(half)
        for c in range(6):
            for z in range(LZ):
                to = slice(z * TLX, (z + 1) * TLX)
                send_buf[rnd, half, 0, c, to, :] = src[c, z, 1, 0:TLY, lanes]
                send_buf[rnd, half, 1, c, to, :] = src[c, z, TLX, 0:TLY, lanes]
                send_buf[rnd, half, 2, c, to, :] = src[c, z, 1:TLX + 1, 0, lanes]
                send_buf[rnd, half, 3, c, to, :] = src[c, z, 1:TLX + 1, TLY - 1, lanes]
        turn(rnd, half, 1, lkx, 0)
        turn(rnd, half, 3, lky, 1)

    def unpack(dst, rnd, half):
        lanes = lanes_of(half)
        for c in range(6):
            for z in range(LZ):
                at = slice(z * TLX, (z + 1) * TLX)
                dst[c, z, TLX + 1, 0:TLY, lanes] = recv_buf[rnd, half, 0, c, at, :]
                dst[c, z, 0, 0:TLY, lanes] = recv_buf[rnd, half, 1, c, at, :]
                dst[c, z, 1:TLX + 1, TLY, lanes] = recv_buf[rnd, half, 2, c, at, :]
                dst[c, z, 1:TLX + 1, YP - 1, lanes] = recv_buf[rnd, half, 3, c, at, :]

    flying = {}

    def send(rnd, half):
        flying[rnd, half] = halo_copies(rnd, half)
        for copy in flying[rnd, half]:
            copy.start()

    def receive(rnd, half):
        for copy in flying[rnd, half]:
            copy.wait()

    pack_given(0)
    pl.semaphore_wait(barrier, len(greeted))
    send(0, 0)
    for half in range(1, halves):
        pack_given(half)
        send(0, half)

    zero_pad = jnp.zeros((YP - TLY, nev), F32)
    zero_rows = jnp.zeros((YP, nev), F32)
    for c in range(6):
        for z in range(LZ):
            for layer in (0, TLX + 1):
                fv[c, z, layer, TLY:YP, :] = zero_pad
                ft[c, z, layer] = zero_rows
            for x in range(TLX):
                at = (z * TLX + x) * TLY
                fv[c, z, x + 1, 0:TLY, :] = v_ref[c // 3, c % 3, 0, at:at + TLY, :]
                fv[c, z, x + 1, TLY:YP, :] = zero_pad

    def spread(r, carry):
        at = pl.multiple_of(r * YP, YP)
        block = lkp[r // (TLX + 1), r % (TLX + 1)]
        for k in range(54):
            links[k, pl.ds(at, YP), :] = jnp.broadcast_to(block[:, k:k + 1], (YP, 128))
        return carry

    lax.fori_loop(0, LZ * (TLX + 1), spread, 0)

    lx = TLX * tiles
    ly = TLY * tiles
    gx = (me // tiles) * TLX + pos_ref[0:1, :]
    gy = (me % tiles) * TLY + pos_ref[1:2, :]
    gx = gx + jnp.where(gy >= ly, TLX, 0) - jnp.where(gy < 0, TLX, 0)
    gy = gy - jnp.where(gy >= ly, ly, 0) + jnp.where(gy < 0, ly, 0)
    gx = gx - jnp.where(gx >= lx, lx, 0) + jnp.where(gx < 0, lx, 0)
    mom = mom_ref[...].astype(F32)

    def turns(k, at, extent):
        f = mom[:, k:k + 1] * at.astype(F32) / extent
        return f - jnp.floor(f)

    theta = 2.0 * math.pi * (turns(0, gx, lx) + turns(1, gy, ly) + turns(2, pos_ref[2:3, :], LZ))
    scale = 1.0 / math.sqrt(3.0 * lx * ly * LZ)
    cs[0] = jnp.cos(theta) * scale
    cs[1] = jnp.sin(theta) * scale

    def link(k, z, layer):
        at = pl.multiple_of((z * (TLX + 1) + layer) * YP, YP)
        def one(i):
            return links[18 * k + i, pl.ds(at, YP), :]
        return [[(one(3 * a + b), one(9 + 3 * a + b)) for b in range(3)] for a in range(3)]

    def load(src, z, layer, lanes):
        return [(src[b, z, layer, :, lanes], src[3 + b, z, layer, :, lanes]) for b in range(3)]

    def roll(f, shift):
        return [(pltpu.roll(r, shift, 0), pltpu.roll(i, shift, 0)) for r, i in f]

    def hops(src, z, x, lanes, k):
        f = load(src, z, x + 1, lanes)
        if k == 0:
            return (mat(link(0, z, x + 1), load(src, z, x + 2, lanes)),
                    adj(link(0, z, x), load(src, z, x, lanes)))
        if k == 1:
            u = link(1, z, x + 1)
            return mat(u, roll(f, YP - 1)), roll(adj(u, f), 1)
        other = load(src, 1 - z, x + 1, lanes)
        return mat(link(2, z, x + 1), other), adj(link(2, 1 - z, x + 1), other)

    real_row = row < TLY

    def smear(src, dst, half):
        lanes = lanes_of(half)

        def body(x, carry):
            for z in range(LZ):
                total = None
                for k in range(3):
                    fwd, bwd = hops(src, z, x, lanes, k)
                    term = [(a[0] + b[0], a[1] + b[1]) for a, b in zip(fwd, bwd)]
                    total = term if total is None else [
                        (a[0] + b[0], a[1] + b[1]) for a, b in zip(total, term)]
                f = load(src, z, x + 1, lanes)
                for a in range(3):
                    for p in range(2):
                        new = f[a][p] + KAPPA * (total[a][p] - 6.0 * f[a][p])
                        dst[3 * p + a, z, x + 1, :, lanes] = jnp.where(real_row, new, 0.0)
            return carry

        lax.fori_loop(0, TLX, body, 0)

    for half in range(halves):
        receive(0, half)
        unpack(fv, 0, half)
        smear(fv, fo, half)
        pack(fo, 1, half)
        send(1, half)

    pieces = []
    for c in range(3):
        pieces += [(c, z, x + 1) for z in range(LZ) for x in range(TLX)]
    for c in range(3):
        pieces += [(c, z, layer) for layer in (TLX + 1, 0) for z in range(LZ)]
    pieces += [None] * (2 * LZ)
    per = 128 // YP
    for chunk in range(KHALF // 128):
        mine = pieces[chunk * per:(chunk + 1) * per]
        vr = jnp.concatenate([zero_rows if q is None else fv[q[0], q[1], q[2]] for q in mine], 0)
        vi = jnp.concatenate([zero_rows if q is None else fv[3 + q[0], q[1], q[2]] for q in mine], 0)
        vr = vr.T
        vi = vi.T
        lanes = slice(chunk * 128, (chunk + 1) * 128)
        lanes_i = slice(KHALF + chunk * 128, KHALF + (chunk + 1) * 128)
        for m in range(nmom):
            co = cs[0, m:m + 1, lanes]
            si = cs[1, m:m + 1, lanes]
            ar = co * vr - si * vi
            ai = -(si * vr + co * vi)
            for a, where_to in ((ar, lanes), (ai, lanes_i)):
                hi = a.astype(BF16)
                lh[m * nev:(m + 1) * nev, where_to] = hi
                ll[m * nev:(m + 1) * nev, where_to] = (a - hi.astype(F32)).astype(BF16)

    def put(row_at, half, col, value):
        hi = value.astype(BF16)
        rh[half, pl.ds(row_at, YP), col] = hi
        rl[half, pl.ds(row_at, YP), col] = (value - hi.astype(F32)).astype(BF16)

    def put_complex(row_at, half, s):
        put(row_at, half, slice(0, 128), s[0])
        put(row_at, half, slice(128, 256), s[1])
        put(row_at + KHALF, half, slice(0, 128), -s[1])
        put(row_at + KHALF, half, slice(128, 256), s[0])

    def displace(half):
        lanes = lanes_of(half)
        which = dir_ref[0:1, lanes]

        def body(x, carry):
            for z in range(LZ):
                diffs = []
                for k in range(3):
                    fwd, bwd = hops(ft, z, x, lanes, k)
                    diffs.append([(a[0] - b[0], a[1] - b[1]) for a, b in zip(fwd, bwd)])
                for c in range(3):
                    s = tuple(jnp.where(which == 0, diffs[0][c][p],
                                        jnp.where(which == 1, diffs[1][c][p], diffs[2][c][p]))
                              for p in range(2))
                    put_complex(pl.multiple_of(c * MAIN + (z * TLX + x) * YP, YP), half, s)
            return carry

        lax.fori_loop(0, TLX, body, 0)
        on_x = which == 0
        for z in range(LZ):
            high = adj(link(0, z, TLX), load(ft, z, TLX, lanes))
            low = load(ft, z, 1, lanes)
            for c in range(3):
                base = 3 * MAIN + c * HALO + z * YP
                put_complex(base, half, tuple(jnp.where(on_x, -high[c][p], 0.0) for p in range(2)))
                put_complex(base + LZ * YP, half,
                            tuple(jnp.where(on_x, low[c][p], 0.0) for p in range(2)))
        zero_tail = jnp.zeros((HALO, 256), BF16)
        for base in (KHALF - HALO, 2 * KHALF - HALO):
            rh[half, base:base + HALO, :] = zero_tail
            rl[half, base:base + HALO, :] = zero_tail

    def reversed_bits(o):
        return sum(((o >> s) & 1) << (stages - 1 - s) for s in range(stages))

    got_at = [0]
    bases = [0]
    for s in range(stages):
        got_at.append(got_at[-1] + (n >> (s + 1)))
        bases.append(bases[-1] + bits[s] * (n >> (s + 1)))
    state = {}

    def launch(job, s):
        half, m0, count = job
        size = n >> (s + 1)
        ms = pl.ds(m0, count)
        copy = pltpu.make_async_remote_copy(
            src_ref=part.at[half, ms, pl.ds(bases[s] + (1 - bits[s]) * size, size)],
            dst_ref=got.at[half, ms, pl.ds(got_at[s], size)],
            send_sem=rs_send.at[half, m0, s], recv_sem=rs_recv.at[half, m0, s],
            device_id={"site": partners[s]}, device_id_type=pl.DeviceIdType.MESH)
        copy.start()
        state[job] = (s, copy)

    def advance(job):
        s, copy = state.pop(job)
        half, m0, count = job
        copy.wait()
        size = n >> (s + 1)
        keep = pl.ds(bases[s + 1], size)
        for m in range(m0, m0 + count):
            summed = part[half, m, keep] + got[half, m, got_at[s]:got_at[s] + size]
            if s + 1 < stages:
                part[half, m, keep] = summed
            else:
                lanes = lanes_of(half)
                out_ref[:, m, 0, lanes] = summed[0, :, 0:128]
                out_ref[:, m, 1, lanes] = summed[0, :, 128:256]
        if s + 1 < stages:
            launch(job, s + 1)

    def advance_all():
        for job in list(state):
            advance(job)

    def multiply(job):
        half, m0, count = job
        take = slice(m0 * nev, (m0 + count) * nev)
        prod = jnp.dot(lh[take, :], rh[half], preferred_element_type=F32)
        prod = prod + jnp.dot(lh[take, :], rl[half], preferred_element_type=F32)
        prod = prod + jnp.dot(ll[take, :], rh[half], preferred_element_type=F32)
        for m in range(count):
            for o in range(n):
                at = m * nev + o * rows
                part[half, m0 + m, reversed_bits(o)] = prod[at:at + rows, :]

    for half in range(halves):
        receive(1, half)
        unpack(fo, 1, half)
        smear(fo, ft, half)
        advance_all()
        displace(half)
        group = 1 if half == halves - 1 else 2
        for m0 in range(0, nmom, group):
            job = (half, m0, min(group, nmom - m0))
            multiply(job)
            advance_all()
            launch(job, 0)
    while state:
        advance_all()


def site_table():
    ys = np.arange(YP)
    ys[YP - 1] = -1
    spots = [(x, y, z) for z in range(LZ) for x in range(TLX) for y in ys] * 3
    spots += [(x, y, z) for x in (TLX, -1) for z in range(LZ) for y in ys] * 4
    return np.array(spots, np.int32).T


def on_device(vectors, links, momenta, directions):
    n = lax.axis_size("site")
    tiles = math.isqrt(n)
    nev = vectors.shape[-1]
    nmom = momenta.shape[0]
    rows = nev // n
    stages = n.bit_length() - 1
    halves = nev // 128
    vmem = pl.BlockSpec(memory_space=pltpu.VMEM)
    ext = pltpu.VMEM((6, LZ, TLX + 2, YP, nev), F32)
    return pl.pallas_call(
        functools.partial(kernel, n, tiles, nmom),
        out_shape=jax.ShapeDtypeStruct((rows, nmom, 2, nev), F32),
        in_specs=[vmem] * 5,
        out_specs=vmem,
        scratch_shapes=[
            ext, ext, ext,
            pltpu.VMEM((54, LZ * (TLX + 1) * YP, 128), F32),
            pltpu.VMEM((128, 384), F32),
            pltpu.VMEM((384, 128), F32),
            pltpu.VMEM((LZ, TLX + 1, YP, 128), F32),
            pltpu.VMEM((SIDE, 128), F32),
            pltpu.VMEM((SIDE, 128), F32),
            pltpu.VMEM((2, nmom, KHALF), F32),
            pltpu.VMEM((2, halves, 4, 6, SIDE, 128), F32),
            pltpu.VMEM((2, halves, 4, 6, SIDE, 128), F32),
            pltpu.VMEM((nmom * nev, 2 * KHALF), BF16),
            pltpu.VMEM((nmom * nev, 2 * KHALF), BF16),
            pltpu.VMEM((halves, 2 * KHALF, 256), BF16),
            pltpu.VMEM((halves, 2 * KHALF, 256), BF16),
            pltpu.VMEM((halves, nmom, n, rows, 256), F32),
            pltpu.VMEM((halves, nmom, n, rows, 256), F32),
            pltpu.SemaphoreType.DMA((2, halves, 4)),
            pltpu.SemaphoreType.DMA((2, halves, 4)),
            pltpu.SemaphoreType.DMA((halves, nmom, stages)),
            pltpu.SemaphoreType.DMA((halves, nmom, stages)),
        ],
        compiler_params=pltpu.CompilerParams(
            collective_id=0, has_side_effects=True, vmem_limit_bytes=60 * 1024 * 1024),
    )(vectors, links.reshape(54, SIDE * TLY), jnp.asarray(site_table()), momenta,
      directions.reshape(1, nev))


def solution(mesh):
    placed = (
        P("grp", None, "site", None, None),
        P("grp", None, None, None, "site", None),
        P(),
        P(),
    )
    return jax.shard_map(
        on_device,
        mesh=mesh,
        in_specs=placed,
        out_specs=P("site", "grp", None, None),
        check_vma=False,
    )
```

time: 92.4 us -> 84.1 us (0.910)
  local copies, waits for them, and re-layouts: 8.42 us -> 2.25 us
  other arithmetic: 2.64 us -> 1.12 us
    reshape x5 -> x1, local copies, waits for them, and re-layouts: 2.61 us -> 0.68 us  [on_device(): links.reshape(54, SIDE * TLY)]
    pad x3 -> x0, local copies, waits for them, and re-layouts: 1.9 us -> none  [the longest x1 0.69 us: on_device(): lk = jnp.pad(flat.reshape(LZ * (TLX + 1) * YP, 54), ((0, 0), (0, 74)))]
    unnamed x0 -> x1, local copies, waits for them, and re-layouts: none -> 1.57 us
    slice x3 -> x0, local copies, waits for them, and re-layouts: 1.39 us -> none  [the longest x1 1.01 us: on_device(): frac = (mom[:, 0] * gx % lx).astype(F32) / lx]
    another operation x7 -> x0, local copies, waits for them, and re-layouts: 1.08 us -> none  [the longest x1 0.75 us: on_device(): flat = local.reshape(54, LZ, TLX, TLY).transpose(1, 2, 3, 0)]
where the time goes in v2:
time: 84.1 us; the launch traced here: 83.9 us
  Pallas kernels  80.6 us (96%)
  local copies, waits for them, and re-layouts  2.25 us (3%)
  other arithmetic  1.12 us (1%)
    pallas_call x1, Pallas kernels, on_device(): pl.pallas_call(functools.partial(kernel, n, tiles, nmom), out_shape=jax.S...  80.6 us

profile of v2, /device:TPU:0, one launch (start us, length us, event | category | flops | bytes accessed | tf_op | source)
XLA Modules:
  0.0 83.9 jit_solution(9353833011359081305)
XLA Ops:
  0.0 1.1 %reduce = f32[3,2,3,3,288]{4,3,2,1,0:T(4,128)S(1)} reduce(f32[3,2,3,3,1,288]{5,4,3,2,1,0:T(1,128)} %param.6, f32[]{:T(128)} %constant.5), dimensions={4}, to_apply=%param.6.reduce_sub_computation | reduce | bytes 124420 | tf_op args[1]
  1.1 0.7 reshape.6.lk_ref
  1.8 80.6 %shard_map.55 = f32[16,4,2,256]{3,2,1,0:T(2,128)} custom-call(f32[2,3,1,288,256]{4,3,2,1,0:T(8,128)} %v_ref.1, f32[54,288]{1,0:T(8,128)} %reshape.6.lk_ref, s32[3,1408]{1,0:T(4,128)} %constant.2.clone.pos_ref, s32[4,3]{1,0:T(4,128)} %mom_ref.1, s32[1,256]{1,0:T(1,128)} %bitcast.1), custom_call_target="tpu_custom_call" | custom-call | tf_op jit(solution)/shard_map/pallas_call | solution.py:428
  82.4 1.6 %copy.8 = f32[16,4,2,256]{3,2,1,0:T(2,128)} copy(f32[16,4,2,256]{3,2,1,0:T(2,128)} %shard_map.55) | data formatting | bytes 262144

commit v3 on v2

--- a/solution.py
+++ b/solution.py
@@ -53,7 +53,7 @@
 
 
 def kernel(n, tiles, nmom, v_ref, lk_ref, pos_ref, mom_ref, dir_ref, out_ref,
-           fv, fo, ft, links, lkw, lkt, lkp, lkx, lky, cs, send_buf, recv_buf, lh, ll, rh, rl,
+           fv, fo, ft, ms, md, bh, bl, lkw, lkt, lkp, lkx, lky, cs, send_buf, recv_buf, lh, ll, rh, rl,
            part, got, send_sem, recv_sem, rs_send, rs_recv):
     nev = v_ref.shape[-1]
     halves = nev // 128
@@ -184,20 +184,76 @@
         for z in range(LZ):
             for layer in (0, TLX + 1):
                 fv[c, z, layer, TLY:YP, :] = zero_pad
+                fo[c, z, layer, TLY:YP, :] = zero_pad
                 ft[c, z, layer] = zero_rows
             for x in range(TLX):
                 at = (z * TLX + x) * TLY
                 fv[c, z, x + 1, 0:TLY, :] = v_ref[c // 3, c % 3, 0, at:at + TLY, :]
                 fv[c, z, x + 1, TLY:YP, :] = zero_pad
 
-    def spread(r, carry):
-        at = pl.multiple_of(r * YP, YP)
-        block = lkp[r // (TLX + 1), r % (TLX + 1)]
-        for k in range(54):
-            links[k, pl.ds(at, YP), :] = jnp.broadcast_to(block[:, k:k + 1], (YP, 128))
+    pad_rows = jnp.zeros((128 - 6 * YP, nev), BF16)
+    for z in range(LZ):
+        for layer in range(TLX + 2):
+            bh[z, layer, 6 * YP:128, :] = pad_rows
+            bl[z, layer, 6 * YP:128, :] = pad_rows
+    segment = lane // YP
+    column = lane % YP
+
+    def masks(shift):
+        return [(segment == b) & (column == (row + shift) % YP) for b in range(6)]
+
+    same, after, before = masks(0), masks(1), masks(YP - 1)
+
+    def spread(block, k):
+        def one(i):
+            return jnp.broadcast_to(block[:, 18 * k + i:18 * k + i + 1], (YP, 128))
+        return [[(one(3 * a + b), one(9 + 3 * a + b)) for b in range(3)] for a in range(3)]
+
+    def chain(where_to, coefs):
+        out = jnp.zeros((YP, 128), F32)
+        for b in range(6):
+            out = jnp.where(where_to[b], coefs[b], out)
+        return out
+
+    def mat_row(u, cp):
+        a = cp % 3
+        if cp < 3:
+            return [u[a][b][0] for b in range(3)] + [-u[a][b][1] for b in range(3)]
+        return [u[a][b][1] for b in range(3)] + [u[a][b][0] for b in range(3)]
+
+    def adj_row(u, cp):
+        a = cp % 3
+        if cp < 3:
+            return [u[b][a][0] for b in range(3)] + [u[b][a][1] for b in range(3)]
+        return [-u[b][a][1] for b in range(3)] + [u[b][a][0] for b in range(3)]
+
+    def put_matrix(dst, z, x, cp, blocks):
+        for j, block in enumerate(blocks):
+            to = slice(j * 128, (j + 1) * 128)
+            hi = block.astype(BF16)
+            dst[z, x, cp * YP:(cp + 1) * YP, to] = hi
+            dst[z, x, (6 + cp) * YP:(7 + cp) * YP, to] = (block - hi.astype(F32)).astype(BF16)
+
+    def build(x, carry):
+        for z in range(LZ):
+            ux = spread(lkp[z, x + 1], 0)
+            uxm = spread(lkp[z, x], 0)
+            uy = spread(lkp[z, x + 1], 1)
+            uym = spread(pltpu.roll(lkp[z, x + 1], 1, 0), 1)
+            uz = spread(lkp[z, x + 1], 2)
+            uzo = spread(lkp[1 - z, x + 1], 2)
+            for cp in range(6):
+                xb = chain(same, adj_row(uxm, cp))
+                xf = chain(same, mat_row(ux, cp))
+                yf = chain(after, mat_row(uy, cp))
+                yb = chain(before, adj_row(uym, cp))
+                zf = chain(same, mat_row(uz, cp))
+                zb = chain(same, adj_row(uzo, cp))
+                put_matrix(ms, z, x, cp, [xb, xf, yf + yb, zf + zb])
+                put_matrix(md, z, x, cp, [-xb, xf, yf - yb, zf - zb])
         return carry
 
-    lax.fori_loop(0, LZ * (TLX + 1), spread, 0)
+    lax.fori_loop(0, TLX, build, 0)
 
     lx = TLX * tiles
     ly = TLY * tiles
@@ -217,47 +273,47 @@
     cs[0] = jnp.cos(theta) * scale
     cs[1] = jnp.sin(theta) * scale
 
-    def link(k, z, layer):
-        at = pl.multiple_of((z * (TLX + 1) + layer) * YP, YP)
-        def one(i):
-            return links[18 * k + i, pl.ds(at, YP), :]
-        return [[(one(3 * a + b), one(9 + 3 * a + b)) for b in range(3)] for a in range(3)]
-
     def load(src, z, layer, lanes):
         return [(src[b, z, layer, :, lanes], src[3 + b, z, layer, :, lanes]) for b in range(3)]
 
-    def roll(f, shift):
-        return [(pltpu.roll(r, shift, 0), pltpu.roll(i, shift, 0)) for r, i in f]
-
-    def hops(src, z, x, lanes, k):
-        f = load(src, z, x + 1, lanes)
-        if k == 0:
-            return (mat(link(0, z, x + 1), load(src, z, x + 2, lanes)),
-                    adj(link(0, z, x), load(src, z, x, lanes)))
-        if k == 1:
-            u = link(1, z, x + 1)
-            return mat(u, roll(f, YP - 1)), roll(adj(u, f), 1)
-        other = load(src, 1 - z, x + 1, lanes)
-        return mat(link(2, z, x + 1), other), adj(link(2, 1 - z, x + 1), other)
+    def split(src, half):
+        lanes = lanes_of(half)
+
+        def body(layer, carry):
+            for z in range(LZ):
+                for c in range(6):
+                    f = src[c, z, layer, :, lanes]
+                    hi = f.astype(BF16)
+                    bh[z, layer, c * YP:(c + 1) * YP, lanes] = hi
+                    bl[z, layer, c * YP:(c + 1) * YP, lanes] = (f - hi.astype(F32)).astype(BF16)
+            return carry
+
+        lax.fori_loop(0, TLX + 2, body, 0)
+
+    def near(src, z, x, lanes):
+        return [src[z, x, :, lanes], src[z, x + 2, :, lanes],
+                src[z, x + 1, :, lanes], src[1 - z, x + 1, :, lanes]]
+
+    def times(matrix, z, x, cols, high, low):
+        count = 6 * YP
+        both = jnp.dot(matrix[z, x, :, cols], high, preferred_element_type=F32)
+        rest = jnp.dot(matrix[z, x, 0:count, cols], low, preferred_element_type=F32)
+        return both[0:count] + both[count:] + rest
 
     real_row = row < TLY
 
     def smear(src, dst, half):
         lanes = lanes_of(half)
+        split(src, half)
 
         def body(x, carry):
             for z in range(LZ):
-                total = None
-                for k in range(3):
-                    fwd, bwd = hops(src, z, x, lanes, k)
-                    term = [(a[0] + b[0], a[1] + b[1]) for a, b in zip(fwd, bwd)]
-                    total = term if total is None else [
-                        (a[0] + b[0], a[1] + b[1]) for a, b in zip(total, term)]
-                f = load(src, z, x + 1, lanes)
-                for a in range(3):
-                    for p in range(2):
-                        new = f[a][p] + KAPPA * (total[a][p] - 6.0 * f[a][p])
-                        dst[3 * p + a, z, x + 1, :, lanes] = jnp.where(real_row, new, 0.0)
+                total = times(ms, z, x, slice(0, 512), jnp.concatenate(near(bh, z, x, lanes), 0),
+                              jnp.concatenate(near(bl, z, x, lanes), 0))
+                for c in range(6):
+                    f = src[c, z, x + 1, :, lanes]
+                    new = f + KAPPA * (total[c * YP:(c + 1) * YP] - 6.0 * f)
+                    dst[c, z, x + 1, :, lanes] = jnp.where(real_row, new, 0.0)
             return carry
 
         lax.fori_loop(0, TLX, body, 0)
@@ -309,12 +365,19 @@
         lanes = lanes_of(half)
         which = dir_ref[0:1, lanes]
 
+        split(ft, half)
+
         def body(x, carry):
             for z in range(LZ):
+                high = near(bh, z, x, lanes)
+                low = near(bl, z, x, lanes)
                 diffs = []
-                for k in range(3):
-                    fwd, bwd = hops(ft, z, x, lanes, k)
-                    diffs.append([(a[0] - b[0], a[1] - b[1]) for a, b in zip(fwd, bwd)])
+                for cols, start, stop in ((slice(0, 256), 0, 2), (slice(256, 384), 2, 3),
+                                          (slice(384, 512), 3, 4)):
+                    d = times(md, z, x, cols, jnp.concatenate(high[start:stop], 0),
+                              jnp.concatenate(low[start:stop], 0))
+                    d = [d[c * YP:(c + 1) * YP] for c in range(6)]
+                    diffs.append([(d[c], d[3 + c]) for c in range(3)])
                 for c in range(3):
                     s = tuple(jnp.where(which == 0, diffs[0][c][p],
                                         jnp.where(which == 1, diffs[1][c][p], diffs[2][c][p]))
@@ -325,7 +388,7 @@
         lax.fori_loop(0, TLX, body, 0)
         on_x = which == 0
         for z in range(LZ):
-            high = adj(link(0, z, TLX), load(ft, z, TLX, lanes))
+            high = adj(spread(lkp[z, TLX], 0), load(ft, z, TLX, lanes))
             low = load(ft, z, 1, lanes)
             for c in range(3):
                 base = 3 * MAIN + c * HALO + z * YP
@@ -432,7 +495,10 @@
         out_specs=vmem,
         scratch_shapes=[
             ext, ext, ext,
-            pltpu.VMEM((54, LZ * (TLX + 1) * YP, 128), F32),
+            pltpu.VMEM((LZ, TLX, 12 * YP, 512), BF16),
+            pltpu.VMEM((LZ, TLX, 12 * YP, 512), BF16),
+            pltpu.VMEM((LZ, TLX + 2, 128, nev), BF16),
+            pltpu.VMEM((LZ, TLX + 2, 128, nev), BF16),
             pltpu.VMEM((128, 384), F32),
             pltpu.VMEM((384, 128), F32),
             pltpu.VMEM((LZ, TLX + 1, YP, 128), F32),

time: 84.1 us -> 87.3 us (1.038)
  Pallas kernels: 80.6 us -> 83.7 us
    pallas_call x1, Pallas kernels: 80.6 us -> 83.7 us  [on_device(): pl.pallas_call(functools.partial(kernel, n, tiles, nmom), out_shape=jax.S...]
where the time goes in v3:
time: 87.3 us; the launch traced here: 87.1 us
  Pallas kernels  83.7 us (96%)
  local copies, waits for them, and re-layouts  2.25 us (3%)
  other arithmetic  1.12 us (1%)
    pallas_call x1, Pallas kernels, on_device(): pl.pallas_call(functools.partial(kernel, n, tiles, nmom), out_shape=jax.S...  83.7 us

profile of v3, /device:TPU:0, one launch (start us, length us, event | category | flops | bytes accessed | tf_op | source)
XLA Modules:
  0.0 87.1 jit_solution(3566540272351307444)
XLA Ops:
  0.0 1.1 %reduce = f32[3,2,3,3,288]{4,3,2,1,0:T(4,128)S(1)} reduce(f32[3,2,3,3,1,288]{5,4,3,2,1,0:T(1,128)} %param.6, f32[]{:T(128)} %constant.5), dimensions={4}, to_apply=%param.6.reduce_sub_computation | reduce | bytes 124420 | tf_op args[1]
  1.1 0.7 reshape.6.lk_ref
  1.8 83.7 %shard_map.55 = f32[16,4,2,256]{3,2,1,0:T(2,128)} custom-call(f32[2,3,1,288,256]{4,3,2,1,0:T(8,128)} %v_ref.1, f32[54,288]{1,0:T(8,128)} %reshape.6.lk_ref, s32[3,1408]{1,0:T(4,128)} %constant.2.clone.pos_ref, s32[4,3]{1,0:T(4,128)} %mom_ref.1, s32[1,256]{1,0:T(1,128)} %bitcast.1), custom_call_target="tpu_custom_call" | custom-call | tf_op jit(solution)/shard_map/pallas_call | solution.py:491
  85.5 1.6 %copy.8 = f32[16,4,2,256]{3,2,1,0:T(2,128)} copy(f32[16,4,2,256]{3,2,1,0:T(2,128)} %shard_map.55) | data formatting | bytes 262144

commit v4 on v2

--- a/solution.py
+++ b/solution.py
@@ -53,7 +53,7 @@
 
 
 def kernel(n, tiles, nmom, v_ref, lk_ref, pos_ref, mom_ref, dir_ref, out_ref,
-           fv, fo, ft, links, lkw, lkt, lkp, lkx, lky, cs, send_buf, recv_buf, lh, ll, rh, rl,
+           fv, fo, ft, links, lkw, lkt, lkp, lkx, lky, cs, turned, flat, send_buf, recv_buf, lh, ll, rh, rl,
            part, got, send_sem, recv_sem, rs_send, rs_recv):
     nev = v_ref.shape[-1]
     halves = nev // 128
@@ -120,9 +120,16 @@
             send_buf[rnd, half, slot, a] = g[a][0]
             send_buf[rnd, half, slot, 3 + a] = g[a][1]
 
+    def each(count, body):
+        def step(i, carry):
+            body(i)
+            return carry
+        lax.fori_loop(0, count, step, 0)
+
     def pack_given(half):
         lanes = lanes_of(half)
-        for c in range(6):
+
+        def one(c):
             p, b = c // 3, c % 3
             for z in range(LZ):
                 at = z * TLX * TLY
@@ -135,24 +142,30 @@
                     send_buf[0, half, 2, c, i:i + 1, :] = v_ref[p, b, 0, at + x * TLY:at + x * TLY + 1, lanes]
                     y = at + x * TLY + TLY - 1
                     send_buf[0, half, 3, c, i:i + 1, :] = v_ref[p, b, 0, y:y + 1, lanes]
+
+        each(6, one)
         turn(0, half, 1, lkx, 0)
         turn(0, half, 3, lky, 1)
 
     def pack(src, rnd, half):
         lanes = lanes_of(half)
-        for c in range(6):
+
+        def one(c):
             for z in range(LZ):
                 to = slice(z * TLX, (z + 1) * TLX)
                 send_buf[rnd, half, 0, c, to, :] = src[c, z, 1, 0:TLY, lanes]
                 send_buf[rnd, half, 1, c, to, :] = src[c, z, TLX, 0:TLY, lanes]
                 send_buf[rnd, half, 2, c, to, :] = src[c, z, 1:TLX + 1, 0, lanes]
                 send_buf[rnd, half, 3, c, to, :] = src[c, z, 1:TLX + 1, TLY - 1, lanes]
+
+        each(6, one)
         turn(rnd, half, 1, lkx, 0)
         turn(rnd, half, 3, lky, 1)
 
     def unpack(dst, rnd, half):
         lanes = lanes_of(half)
-        for c in range(6):
+
+        def one(c):
             for z in range(LZ):
                 at = slice(z * TLX, (z + 1) * TLX)
                 dst[c, z, TLX + 1, 0:TLY, lanes] = recv_buf[rnd, half, 0, c, at, :]
@@ -160,6 +173,8 @@
                 dst[c, z, 1:TLX + 1, TLY, lanes] = recv_buf[rnd, half, 2, c, at, :]
                 dst[c, z, 1:TLX + 1, YP - 1, lanes] = recv_buf[rnd, half, 3, c, at, :]
 
+        each(6, one)
+
     flying = {}
 
     def send(rnd, half):
@@ -180,7 +195,7 @@
 
     zero_pad = jnp.zeros((YP - TLY, nev), F32)
     zero_rows = jnp.zeros((YP, nev), F32)
-    for c in range(6):
+    def own(c):
         for z in range(LZ):
             for layer in (0, TLX + 1):
                 fv[c, z, layer, TLY:YP, :] = zero_pad
@@ -190,6 +205,8 @@
                 fv[c, z, x + 1, 0:TLY, :] = v_ref[c // 3, c % 3, 0, at:at + TLY, :]
                 fv[c, z, x + 1, TLY:YP, :] = zero_pad
 
+    each(6, own)
+
     def spread(r, carry):
         at = pl.multiple_of(r * YP, YP)
         block = lkp[r // (TLX + 1), r % (TLX + 1)]
@@ -214,8 +231,11 @@
 
     theta = 2.0 * math.pi * (turns(0, gx, lx) + turns(1, gy, ly) + turns(2, pos_ref[2:3, :], LZ))
     scale = 1.0 / math.sqrt(3.0 * lx * ly * LZ)
-    cs[0] = jnp.cos(theta) * scale
-    cs[1] = jnp.sin(theta) * scale
+    cosine = jnp.cos(theta) * scale
+    sine = jnp.sin(theta) * scale
+    for m in range(nmom):
+        cs[0, m] = cosine[m:m + 1, :]
+        cs[1, m] = sine[m:m + 1, :]
 
     def link(k, z, layer):
         at = pl.multiple_of((z * (TLX + 1) + layer) * YP, YP)
@@ -269,30 +289,47 @@
         pack(fo, 1, half)
         send(1, half)
 
-    pieces = []
-    for c in range(3):
-        pieces += [(c, z, x + 1) for z in range(LZ) for x in range(TLX)]
-    for c in range(3):
-        pieces += [(c, z, layer) for layer in (TLX + 1, 0) for z in range(LZ)]
-    pieces += [None] * (2 * LZ)
+    def left_chunk(at, where):
+        for i in range(128 // YP):
+            c, z, layer = where(i)
+            turned[0, i * YP:(i + 1) * YP, :] = fv[c, z, layer]
+            turned[1, i * YP:(i + 1) * YP, :] = fv[3 + c, z, layer]
+        vr = turned[0].T
+        vi = turned[1].T
+        lanes = pl.ds(pl.multiple_of(at, 128), 128)
+        lanes_i = pl.ds(pl.multiple_of(KHALF + at, 128), 128)
+        flat[0] = vr
+        flat[1] = vi
+
+        def one(m):
+            rows_m = pl.ds(pl.multiple_of(m * nev, nev), nev)
+            co = cs[0, m, :, lanes]
+            si = cs[1, m, :, lanes]
+            re = flat[0]
+            im = flat[1]
+            for a, where_to in ((co * re - si * im, lanes), (-(si * re + co * im), lanes_i)):
+                hi = a.astype(BF16)
+                lh[rows_m, where_to] = hi
+                ll[rows_m, where_to] = (a - hi.astype(F32)).astype(BF16)
+
+        each(nmom, one)
+
     per = 128 // YP
-    for chunk in range(KHALF // 128):
-        mine = pieces[chunk * per:(chunk + 1) * per]
-        vr = jnp.concatenate([zero_rows if q is None else fv[q[0], q[1], q[2]] for q in mine], 0)
-        vi = jnp.concatenate([zero_rows if q is None else fv[3 + q[0], q[1], q[2]] for q in mine], 0)
-        vr = vr.T
-        vi = vi.T
-        lanes = slice(chunk * 128, (chunk + 1) * 128)
-        lanes_i = slice(KHALF + chunk * 128, KHALF + (chunk + 1) * 128)
-        for m in range(nmom):
-            co = cs[0, m:m + 1, lanes]
-            si = cs[1, m:m + 1, lanes]
-            ar = co * vr - si * vi
-            ai = -(si * vr + co * vi)
-            for a, where_to in ((ar, lanes), (ai, lanes_i)):
-                hi = a.astype(BF16)
-                lh[m * nev:(m + 1) * nev, where_to] = hi
-                ll[m * nev:(m + 1) * nev, where_to] = (a - hi.astype(F32)).astype(BF16)
+
+    def main_chunk(q):
+        def where(i):
+            at = (q % 3) * per + i
+            return q // 3, at // TLX, at % TLX + 1
+        left_chunk(q * 128, where)
+
+    def halo_chunk(q):
+        def where(i):
+            at = q * per + i
+            return jnp.minimum(at // (2 * LZ), 2), at % LZ, (TLX + 1) * (1 - (at // LZ) % 2)
+        left_chunk(3 * MAIN + q * 128, where)
+
+    each(3 * MAIN // 128, main_chunk)
+    each(4 * HALO // 128, halo_chunk)
 
     def put(row_at, half, col, value):
         hi = value.astype(BF16)
@@ -366,14 +403,19 @@
         size = n >> (s + 1)
         keep = pl.ds(bases[s + 1], size)
         for m in range(m0, m0 + count):
-            summed = part[half, m, keep] + got[half, m, got_at[s]:got_at[s] + size]
-            if s + 1 < stages:
-                part[half, m, keep] = summed
-            else:
+            if s + 1 == stages:
+                summed = part[half, m, keep] + got[half, m, got_at[s]:got_at[s] + size]
                 lanes = lanes_of(half)
                 out_ref[:, m, 0, lanes] = summed[0, :, 0:128]
                 out_ref[:, m, 1, lanes] = summed[0, :, 128:256]
         if s + 1 < stages:
+            def add(i):
+                m = m0 + i // size
+                o = i % size
+                at = bases[s + 1] + o
+                part[half, m, at] = part[half, m, at] + got[half, m, got_at[s] + o]
+            each(count * size, add)
+        if s + 1 < stages:
             launch(job, s + 1)
 
     def advance_all():
@@ -382,14 +424,17 @@
 
     def multiply(job):
         half, m0, count = job
-        take = slice(m0 * nev, (m0 + count) * nev)
-        prod = jnp.dot(lh[take, :], rh[half], preferred_element_type=F32)
-        prod = prod + jnp.dot(lh[take, :], rl[half], preferred_element_type=F32)
-        prod = prod + jnp.dot(ll[take, :], rh[half], preferred_element_type=F32)
-        for m in range(count):
+
+        def one(i):
+            m = m0 + i
+            take = pl.ds(pl.multiple_of(m * nev, nev), nev)
+            prod = jnp.dot(lh[take, :], rh[half], preferred_element_type=F32)
+            prod = prod + jnp.dot(lh[take, :], rl[half], preferred_element_type=F32)
+            prod = prod + jnp.dot(ll[take, :], rh[half], preferred_element_type=F32)
             for o in range(n):
-                at = m * nev + o * rows
-                part[half, m0 + m, reversed_bits(o)] = prod[at:at + rows, :]
+                part[half, m, reversed_bits(o)] = prod[o * rows:(o + 1) * rows, :]
+
+        each(count, one)
 
     for half in range(halves):
         receive(1, half)
@@ -397,7 +442,7 @@
         smear(fo, ft, half)
         advance_all()
         displace(half)
-        group = 1 if half == halves - 1 else 2
+        group = 2 if half == halves - 1 else nmom
         for m0 in range(0, nmom, group):
             job = (half, m0, min(group, nmom - m0))
             multiply(job)
@@ -438,7 +483,9 @@
             pltpu.VMEM((LZ, TLX + 1, YP, 128), F32),
             pltpu.VMEM((SIDE, 128), F32),
             pltpu.VMEM((SIDE, 128), F32),
-            pltpu.VMEM((2, nmom, KHALF), F32),
+            pltpu.VMEM((2, nmom, 1, KHALF), F32),
+            pltpu.VMEM((2, 128, nev), F32),
+            pltpu.VMEM((2, nev, 128), F32),
             pltpu.VMEM((2, halves, 4, 6, SIDE, 128), F32),
             pltpu.VMEM((2, halves, 4, 6, SIDE, 128), F32),
             pltpu.VMEM((nmom * nev, 2 * KHALF), BF16),

time: 84.1 us -> 79.2 us (0.942)
  Pallas kernels: 80.6 us -> 75.6 us
    pallas_call x1, Pallas kernels: 80.6 us -> 75.6 us  [on_device(): pl.pallas_call(functools.partial(kernel, n, tiles, nmom), out_shape=jax.S...]
where the time goes in v4:
time: 79.2 us; the launch traced here: 79 us
  Pallas kernels  75.6 us (95%)
  local copies, waits for them, and re-layouts  2.25 us (3%)
  other arithmetic  1.12 us (1%)
    pallas_call x1, Pallas kernels, on_device(): pl.pallas_call(functools.partial(kernel, n, tiles, nmom), out_shape=jax.S...  75.6 us

profile of v4, /device:TPU:0, one launch (start us, length us, event | category | flops | bytes accessed | tf_op | source)
XLA Modules:
  0.0 79.0 jit_solution(8297951711153161552)
XLA Ops:
  0.0 1.1 %reduce = f32[3,2,3,3,288]{4,3,2,1,0:T(4,128)S(1)} reduce(f32[3,2,3,3,1,288]{5,4,3,2,1,0:T(1,128)} %param.6, f32[]{:T(128)} %constant.5), dimensions={4}, to_apply=%param.6.reduce_sub_computation | reduce | bytes 124420 | tf_op args[1]
  1.1 0.7 reshape.6.lk_ref
  1.8 75.6 %shard_map.55 = f32[16,4,2,256]{3,2,1,0:T(2,128)} custom-call(f32[2,3,1,288,256]{4,3,2,1,0:T(8,128)} %v_ref.1, f32[54,288]{1,0:T(8,128)} %reshape.6.lk_ref, s32[3,1408]{1,0:T(4,128)} %constant.2.clone.pos_ref, s32[4,3]{1,0:T(4,128)} %mom_ref.1, s32[1,256]{1,0:T(1,128)} %bitcast.1), custom_call_target="tpu_custom_call" | custom-call | tf_op jit(solution)/shard_map/pallas_call | solution.py:473
  77.4 1.6 %copy.8 = f32[16,4,2,256]{3,2,1,0:T(2,128)} copy(f32[16,4,2,256]{3,2,1,0:T(2,128)} %shard_map.55) | data formatting | bytes 262144

commit v5 on v4

--- a/solution.py
+++ b/solution.py
@@ -81,7 +81,9 @@
         return slice(half * 128, (half + 1) * 128)
 
     lkw[...] = jnp.zeros_like(lkw)
-    lkw[0:54, 0:SIDE * TLY] = lk_ref[...]
+    for i in range(54):
+        k, p, a, b = i // 18, i // 9 % 2, i // 3 % 3, i % 3
+        lkw[i:i + 1, 0:SIDE * TLY] = lk_ref[k, p, a, b]
     lkt[...] = lkw[...].T
     lane = lax.broadcasted_iota(jnp.int32, (YP, 128), 1)
     row = lax.broadcasted_iota(jnp.int32, (YP, 128), 0)
@@ -406,8 +408,8 @@
             if s + 1 == stages:
                 summed = part[half, m, keep] + got[half, m, got_at[s]:got_at[s] + size]
                 lanes = lanes_of(half)
-                out_ref[:, m, 0, lanes] = summed[0, :, 0:128]
-                out_ref[:, m, 1, lanes] = summed[0, :, 128:256]
+                out_ref[:, 2 * m, lanes] = summed[0, :, 0:128]
+                out_ref[:, 2 * m + 1, lanes] = summed[0, :, 128:256]
         if s + 1 < stages:
             def add(i):
                 m = m0 + i // size
@@ -470,9 +472,9 @@
     halves = nev // 128
     vmem = pl.BlockSpec(memory_space=pltpu.VMEM)
     ext = pltpu.VMEM((6, LZ, TLX + 2, YP, nev), F32)
-    return pl.pallas_call(
+    out = pl.pallas_call(
         functools.partial(kernel, n, tiles, nmom),
-        out_shape=jax.ShapeDtypeStruct((rows, nmom, 2, nev), F32),
+        out_shape=jax.ShapeDtypeStruct((rows, 2 * nmom, nev), F32),
         in_specs=[vmem] * 5,
         out_specs=vmem,
         scratch_shapes=[
@@ -501,8 +503,9 @@
         ],
         compiler_params=pltpu.CompilerParams(
             collective_id=0, has_side_effects=True, vmem_limit_bytes=60 * 1024 * 1024),
-    )(vectors, links.reshape(54, SIDE * TLY), jnp.asarray(site_table()), momenta,
+    )(vectors, links, jnp.asarray(site_table()), momenta,
       directions.reshape(1, nev))
+    return out.reshape(rows, nmom, 2, nev)
 
 
 def solution(mesh):

time: 79.2 us -> 77.5 us (0.979)
  other arithmetic: 1.12 us -> 0 us
    unnamed x1 -> x0, local copies, waits for them, and re-layouts: 1.57 us -> none
    unnamed x1 -> x0, other arithmetic: 1.12 us -> none
    reshape x1, local copies, waits for them, and re-layouts: 0.68 us -> 1.63 us  [on_device(): return out.reshape(rows, nmom, 2, nev)]
where the time goes in v5:
time: 77.5 us; the launch traced here: 77.3 us
  Pallas kernels  75.7 us (98%)
  local copies, waits for them, and re-layouts  1.63 us (2%)
    pallas_call x1, Pallas kernels, on_device(): pl.pallas_call(functools.partial(kernel, n, tiles, nmom), out_shape=jax.S...  75.7 us
    reshape x1, local copies, waits for them, and re-layouts, on_device(): return out.reshape(rows, nmom, 2, nev)  1.63 us

profile of v5, /device:TPU:0, one launch (start us, length us, event | category | flops | bytes accessed | tf_op | source)
XLA Modules:
  0.0 77.3 jit_solution(8353442504948132938)
XLA Ops:
  0.0 75.7 %shard_map.55 = f32[16,8,256]{2,1,0:T(8,128)} custom-call(f32[2,3,1,288,256]{4,3,2,1,0:T(8,128)} %v_ref.1, f32[3,2,3,3,1,288]{5,4,3,2,1,0:T(1,128)} %lk_ref.1, s32[3,1408]{1,0:T(4,128)} %constant.2.clone.pos_ref, s32[4,3]{1,0:T(4,128)} %mom_ref.1, s32[1,256]{1,0:T(1,128)} %bitcast.1), custom_call_target="tpu_custom_call" | custom-call | tf_op jit(solution)/shard_map/pallas_call | solution.py:475
  75.7 1.6 %reshape.7 = f32[16,4,2,256]{3,2,1,0:T(2,128)} reshape(f32[16,8,256]{2,1,0:T(8,128)} %shard_map.55) | data formatting | bytes 262144 | tf_op jit(solution)/shard_map/reshape | solution.py:508
